TPU v7x, 32 devices: a whole 2x2x4 slice. The times are simulated.
32 devices in a mesh: pool: 8 (over z, x), tp: 4 (over y, core).
Axes of the slice: x: 2, y: 2, z: 4, core: 2. Of those that a mesh axis runs over, the one named last changes fastest.
Arguments:
- hidden_rows: bfloat16 [1024, 8192], P('pool', 'tp'), may hold values from -6 to 6
- kv_weight: bfloat16 [8192, 1024], P('tp', 'pool'), may hold values from -0.0625 to 0.0625
- queries: bfloat16 [1024, 4096], P('pool', 'tp'), may hold values from -5 to 5
- cache_table: bfloat16 [64, 128, 1024], P('pool', None, 'tp'), may hold values from -5 to 5
- retrieval: int32 [8, 4], P('pool'), may hold values from 0 to 63, as said below
- pattern: int32 [8, 2, 4], P('pool'), may hold values 0 or 1
Outputs:
- attended: bfloat16 [1024, 4096], P('pool', 'tp')
- fresh_kv: bfloat16 [1024, 1024], P('pool', 'tp')
Inputs may be any that keep to these rules, and one draw needn't show every extreme that they name: `retrieval`: each request names 4 blocks held by 4 different devices (block b is held by device b // 8); one device, drawn from the seed, holds a block named by every request.
All inputs are finite; a program needn't handle non-finite values. No bound on the sum of `pattern` on one device may be relied on, other than what follows from the above.
Results may differ from a plain program's by a relative error of at most 0.025.
Values may be sent and summed in bfloat16 or wider, within the bound.
A program may use at most 192 MiB of HBM per device.

v0:
```python
import math

import jax
import jax.numpy as jnp
from jax import lax
from jax.sharding import PartitionSpec as P

HD = 128
QH = 32
KVH = 4
BLK = 128
RBLK = 64


def rows_by_keys(left, right):
    return lax.dot_general(
        left, right, (((1,), (1,)), ((), ())), preferred_element_type=jnp.float32
    )


def body(hidden_rows, kv_weight, queries, cache_table, retrieval, pattern):
    partial_kv = jnp.dot(
        hidden_rows,
        lax.all_gather(kv_weight, "pool", axis=1, tiled=True),
        preferred_element_type=jnp.float32,
    )
    fresh = lax.psum_scatter(partial_kv.astype(jnp.bfloat16), "tp", scatter_dimension=1, tiled=True)
    wanted = retrieval[0]
    blocks_dev = cache_table.shape[0]
    npool = lax.axis_size("pool")
    owners = wanted // blocks_dev
    local = wanted % blocks_dev
    hits = (owners[:, None] == jnp.arange(npool, dtype=jnp.int32)[None, :]).astype(jnp.int32)
    request = jnp.sum(hits * (local + 1)[:, None], axis=0)
    incoming = lax.all_to_all(
        request.reshape(npool, 1), "pool", split_axis=0, concat_axis=0, tiled=True
    ).reshape(npool)
    reply = jnp.zeros((npool,) + cache_table.shape[1:], jnp.bfloat16)
    for slot in range(blocks_dev):
        reply = jnp.where((incoming == slot + 1)[:, None, None], cache_table[slot][None], reply)
    arrived = lax.all_to_all(reply, "pool", split_axis=0, concat_axis=0, tiled=True)
    fetched = jnp.take(arrived, owners, axis=0)
    count = hidden_rows.shape[0]
    fetch_count = wanted.shape[0]
    group = QH // KVH
    scale = float(HD) ** (-0.5)
    local_heads = fresh.shape[1] // (2 * HD)
    width = fetched.shape[2]
    per_step = math.gcd(fetch_count, 8)
    steps_count = fetch_count // per_step
    grouped = fetched.reshape(steps_count, per_step * BLK, width)
    pat_steps = jnp.transpose(
        pattern[0].reshape(pattern.shape[1], steps_count, per_step), (1, 0, 2)
    )
    token_of_row = jnp.arange(count * group) // group
    block_of_row = token_of_row // RBLK
    row_blocks = block_of_row[:, None, None] == jnp.arange(pattern.shape[1])[None, :, None]
    near_mask = token_of_row[:, None] >= jnp.arange(count)[None, :]
    q_heads = queries.reshape(count, local_heads, group * HD)
    q_rows = q_heads[:, 0].reshape(count * group, HD)
    near_keys = fresh[:, 0:HD]
    near_vals = fresh[:, HD : 2 * HD]
    near_scores = rows_by_keys(q_rows, near_keys) * scale
    top = jnp.max(jnp.where(near_mask, near_scores, -1e30), axis=1)
    weights = jnp.where(near_mask, jnp.exp(near_scores - top[:, None]), 0.0)
    total = jnp.sum(weights, axis=1)
    numer = jnp.dot(weights.astype(jnp.bfloat16), near_vals, preferred_element_type=jnp.float32)

    def visit(carry, items):
        top_now, total_now, numer_now = carry
        block_rows, pat_now = items
        keys = block_rows[:, 0:HD]
        vals = block_rows[:, HD : 2 * HD]
        scores = rows_by_keys(q_rows, keys) * scale
        row_pat = jnp.any(row_blocks & (pat_now[None] != 0), axis=1)
        mask = jnp.repeat(row_pat, BLK, axis=1)
        top_new = jnp.maximum(top_now, jnp.max(jnp.where(mask, scores, -1e30), axis=1))
        weights_now = jnp.where(mask, jnp.exp(scores - top_new[:, None]), 0.0)
        factor = jnp.exp(top_now - top_new)
        total_new = total_now * factor + jnp.sum(weights_now, axis=1)
        numer_new = numer_now * factor[:, None] + jnp.dot(
            weights_now.astype(jnp.bfloat16), vals, preferred_element_type=jnp.float32
        )
        return ((top_new, total_new, numer_new), None)

    (top, total, numer), unused = lax.scan(visit, (top, total, numer), (grouped, pat_steps))
    results = (numer / total[:, None]).reshape(count, group * HD)
    attended = results.astype(jnp.bfloat16)
    return (attended, fresh)


def solution(mesh):
    placed = (
        P("pool", "tp"),
        P("tp", "pool"),
        P("pool", "tp"),
        P("pool", None, "tp"),
        P("pool", None),
        P("pool", None, None),
    )
    return jax.shard_map(
        body,
        mesh=mesh,
        in_specs=placed,
        out_specs=(P("pool", "tp"), P("pool", "tp")),
        check_vma=False,
    )
```

profile of v0, /device:TPU:0, one launch (start us, length us, event | category | flops | bytes accessed | tf_op | source)
XLA Modules:
  0.0 130.7 jit_solution(7412240481732382975)
XLA Ops:
  7.2 0.0 copy-start
  7.2 0.0 copy-start.3
  7.2 0.0 copy-start.1
  7.2 0.0 all-gather.2.cloned.1.call-start
  7.2 0.7 all-gather.2.cloned.1.call-update
  7.9 0.7 fusion.23
  8.6 0.7 compare_and_fusion
  9.3 0.1 select_reduce_fusion.1
  9.4 0.7 copy.10
  10.0 7.3 %all-to-all-start = ((s32[8,1,1]{2,1,0:T(1,128)}), s32[8,1,1]{2,1,0:T(1,128)S(1)}, u32[]{:S(2)}, u32[]{:S(2)}) async-start(s32[8,1,1]{2,1,0:T(1,128)} %copy.10), calls=%async_computation.1 | async-start | bytes 8192 | tf_op jit(solution)/shard_map/all_to_all | solution.py:35
  17.3 0.7 compare_bitcast_fusion
  18.0 1.1 slice_bitcast_fusion.7
  19.1 0.1 and_reduce_fusion
  19.2 4.5 %all-to-all-done = s32[8,1,1]{2,1,0:T(1,128)S(1)} async-done(((s32[8,1,1]{2,1,0:T(1,128)}), s32[8,1,1]{2,1,0:T(1,128)S(1)}, u32[]{:S(2)}, u32[]{:S(2)}) %all-to-all-start) | async-done | bytes 64 | tf_op jit(solution)/shard_map/all_to_all | solution.py:35
  23.7 1.3 compare_reduce_fusion.7
  24.9 1.1 select_select_fusion
  26.1 3.5 %all-to-all-start.1 = ((bf16[8,128,256]{2,1,0:T(8,128)(2,1)}), bf16[8,128,256]{2,1,0:T(8,128)(2,1)S(1)}, u32[]{:S(2)}, u32[]{:S(2)}) async-start(bf16[8,128,256]{2,1,0:T(8,128)(2,1)} %select_select_fusion), calls=%async_computation.2 | async-start | bytes 1048576 | tf_op jit(solution)/shard_map/all_to_all | solution.py:41
  29.6 0.0 reduce-scatter.2.cloned.1.call-start
  29.6 0.0 copy-done.1
  29.6 0.1 reshape_squeeze_reshape.3
  29.8 0.0 copy-done.3
  29.8 68.7 %all-gather.2.cloned.1.call-done = bf16[2048,1024]{1,0:T(8,128)(2,1)} async-done(((bf16[2048,128]{1,0:T(8,128)(2,1)}), bf16[2048,1024]{1,0:T(8,128)(2,1)}) %all-gather.2.cloned.1.call-update) | async-done | bytes 4194320 | tf_op jit(solution)/shard_map/all_gather | solution.py:24
  98.5 0.0 copy-done
  98.5 3.6 %convolution_convert_fusion = bf16[128,1024]{1,0:T(8,128)(2,1)} fusion(bf16[128,2048]{1,0:T(8,128)(2,1)S(1)} %copy-done, bf16[2048,1024]{1,0:T(8,128)(2,1)} %all-gather.2.cloned.1.call-done), kind=kOutput, calls=%fused_computation.14 | convolution fusion | flops 537001984 | bytes 4980736 | tf_op jit(solution)/shard_map/dot_general | solution.py:22
  102.1 0.0 reduce-scatter.2.cloned.1.call-update
  102.1 0.1 broadcast_bitcast_fusion
  102.2 0.0 all-to-all-done.1
  102.2 0.6 gather_fusion
  102.8 0.1 bitcast_select_fusion.2
  102.9 0.5 fusion
  103.4 17.1 %reduce-scatter.2.cloned.1.call-done = bf16[128,256]{1,0:T(8,128)(2,1)} async-done(((bf16[128,1024]{1,0:T(8,128)(2,1)}), bf16[128,256]{1,0:T(8,128)(2,1)}) %reduce-scatter.2.cloned.1.call-update) | async-done | bytes 65552 | tf_op jit(solution)/shard_map/reduce_scatter | solution.py:27
  120.5 0.0 copy-start.2
  120.5 1.1 select_reduce_fusion
  121.6 0.1 fusion.7
  121.7 0.5 fusion.3
  122.2 0.0 copy-done.2
  122.2 0.3 convolution_multiply_fusion
  122.6 0.5 fusion.6
  123.1 0.8 convert_element_type.21
  (7 shorter events, 0.1 us)
Async XLA Ops:
  7.2 91.3 %copy-start = (bf16[128,2048]{1,0:T(8,128)(2,1)S(1)}, bf16[128,2048]{1,0:T(8,128)(2,1)}, u32[]{:S(2)}) copy-start(bf16[128,2048]{1,0:T(8,128)(2,1)} %param.6) | copy-start | bytes 1572868
  7.2 22.6 %copy-start.3 = (s32[1,4]{1,0:T(1,128)S(1)}, s32[1,4]{1,0:T(1,128)}, u32[]{:S(2)}) copy-start(s32[1,4]{1,0:T(1,128)} %param.10) | copy-start | bytes 52
  7.2 22.4 %copy-start.1 = (bf16[128,1024]{1,0:T(8,128)(2,1)S(1)}, bf16[128,1024]{1,0:T(8,128)(2,1)}, u32[]{:S(2)}) copy-start(bf16[128,1024]{1,0:T(8,128)(2,1)} %param.8) | copy-start | bytes 786436
  7.2 91.3 %all-gather.2.cloned.1.call-start = ((), (), s32[]{:S(2)}) async-start(), calls=%async_computation.3 | async-start | bytes 4718592 | tf_op jit(solution)/shard_map/all_gather | solution.py:24
  10.0 13.7 %all-to-all-start = ((s32[8,1,1]{2,1,0:T(1,128)}), s32[8,1,1]{2,1,0:T(1,128)S(1)}, u32[]{:S(2)}, u32[]{:S(2)}) async-start(s32[8,1,1]{2,1,0:T(1,128)} %copy.10), calls=%async_computation.1 | async-start | bytes 8192 | tf_op jit(solution)/shard_map/all_to_all | solution.py:35
  26.1 76.1 %all-to-all-start.1 = ((bf16[8,128,256]{2,1,0:T(8,128)(2,1)}), bf16[8,128,256]{2,1,0:T(8,128)(2,1)S(1)}, u32[]{:S(2)}, u32[]{:S(2)}) async-start(bf16[8,128,256]{2,1,0:T(8,128)(2,1)} %select_select_fusion), calls=%async_computation.2 | async-start | bytes 1048576 | tf_op jit(solution)/shard_map/all_to_all | solution.py:41
  29.6 90.9 %reduce-scatter.2.cloned.1.call-start = ((), (), s32[]{:S(2)}) async-start(), calls=%async_computation.4 | async-start | bytes 327680 | tf_op jit(solution)/shard_map/reduce_scatter | solution.py:27
  120.5 1.7 %copy-start.2 = (bf16[128,256]{1,0:T(8,128)(2,1)S(1)}, bf16[128,256]{1,0:T(8,128)(2,1)}, u32[]{:S(2)}) copy-start(bf16[128,256]{1,0:T(8,128)(2,1)} %reduce-scatter.2.cloned.1.call-done) | copy-start | bytes 196612
Sparse Core Ops, SparseCore 0:
  10.1 88.3 all-gather.1
  102.2 18.2 reduce-scatter.1
where the time goes:
time: 131 us
  waiting for transfers between devices  91 us (69%)
  between operations  14.2 us (11%)
  starting transfers between devices  10.8 us (8%)
  matrix products  5.98 us (5%)
  other arithmetic  5.35 us (4%)
  local copies, waits for them, and re-layouts  3.37 us (3%)
    all_gather x1, waiting for transfers between devices, body(): lax.all_gather(kv_weight, 'pool', axis=1, tiled=True)  68.7 us
    reduce_scatter x1, waiting for transfers between devices, body(): lax.psum_scatter(partial_kv.astype(jnp.bfloat16), 'tp', scatter_dimension...  17.1 us
    all_to_all x1, starting transfers between devices, body(): lax.all_to_all(request.reshape(npool, 1), 'pool', split_axis=0, concat_ax...  7.27 us
    all_to_all x1, waiting for transfers between devices, body(): lax.all_to_all(request.reshape(npool, 1), 'pool', split_axis=0, concat_ax...  4.49 us
    dot_general x1, matrix products, body(): jnp.dot(hidden_rows, lax.all_gather(kv_weight, 'pool', axis=1, tiled=True...  3.61 us
    all_to_all x1, starting transfers between devices, body(): lax.all_to_all(reply, 'pool', split_axis=0, concat_axis=0, tiled=True)  3.49 us
  transfers between devices with their start and end apart: 4, of which 3 were waited for; matrix products, arithmetic and copies ran while one was open for 9% of the time, Pallas kernels for 0%

commit v1 on v0

--- a/solution.py
+++ b/solution.py
@@ -3,6 +3,8 @@
 import jax
 import jax.numpy as jnp
 from jax import lax
+from jax.experimental import pallas as pl
+from jax.experimental.pallas import tpu as pltpu
 from jax.sharding import PartitionSpec as P
 
 HD = 128
@@ -89,6 +91,256 @@
     return (attended, fresh)
 
 
+MESH = pl.DeviceIdType.MESH
+
+
+def kernel(hid, wgt, q_ref, cache, retr, pat, att, fresh, hbuf, wbuf, pbuf, part, msg_out, msg_in,
+           reply, arrived, kcat, vcat, h_recv, h_send, w_recv, w_send, m_recv, m_send, f_recv, f_send,
+           s_recv, s_send):
+    npool = 8
+    blocks_dev = cache.shape[0]
+    fetch = retr.shape[1]
+    rows = hid.shape[0]
+    me = lax.axis_index("pool")
+    t = lax.axis_index("tp")
+    z, x = lax.div(me, 2), lax.rem(me, 2)
+    a, b = lax.div(z, 2), lax.rem(z, 2)
+    y = lax.div(t, 2)
+    pair = (2 * a + 1 - b) * 2 + x
+    other = z * 2 + 1 - x
+    far = (2 - a) * 2 + x
+
+    def remote(src, dst, ssem, rsem, pool, tp=None):
+        where = {"pool": pool} if tp is None else {"pool": pool, "tp": tp}
+        return pltpu.make_async_remote_copy(
+            src_ref=src, dst_ref=dst, send_sem=ssem, recv_sem=rsem, device_id=where, device_id_type=MESH
+        )
+
+    def rows_at(slot, count=1):
+        return pl.ds(pl.multiple_of(slot * rows, rows), count * rows)
+
+    def cols_at(slot):
+        return pl.ds(pl.multiple_of(slot * HD, HD), HD)
+
+    own_slot = b * 2 + x
+    pair_slot = (1 - b) * 2 + x
+    own_h = pltpu.make_async_copy(hid, hbuf.at[rows_at(own_slot)], h_recv.at[own_slot])
+    own_h.start()
+
+    @pl.when(a == b)
+    def _():
+        pltpu.make_async_copy(wgt, wbuf.at[:, cols_at(b)], w_recv.at[b]).start()
+
+    barrier = pltpu.get_barrier_semaphore()
+    for k in range(1, npool):
+        pl.semaphore_signal(barrier, inc=1, device_id={"pool": lax.rem(me + k, npool)}, device_id_type=MESH)
+    for sx in range(2):
+        for k in range(1, 4):
+            pl.semaphore_signal(
+                barrier, inc=1,
+                device_id={"pool": (2 * a + y) * 2 + sx, "tp": lax.rem(t + k, 4)}, device_id_type=MESH,
+            )
+    pl.semaphore_wait(barrier, npool - 1 + jnp.where(y == b, 4, 8))
+
+    h_pair = remote(hid, hbuf.at[rows_at(own_slot)], h_send.at[0], h_recv.at[own_slot], pair)
+    h_other = remote(hid, hbuf.at[rows_at(own_slot)], h_send.at[1], h_recv.at[own_slot], other)
+    w_far = remote(wgt, wbuf.at[:, cols_at(b)], w_send.at[0], w_recv.at[b], far)
+    w_near = remote(wgt, wbuf.at[:, cols_at(b)], w_send.at[1], w_recv.at[b], pair)
+
+    wanted = [retr[0, f] for f in range(fetch)]
+    owners = [lax.div(v, blocks_dev) for v in wanted]
+    locals_ = [lax.rem(v, blocks_dev) for v in wanted]
+
+    def slot_at(owner):
+        total = jnp.int32(0)
+        for f in range(fetch):
+            total = total + jnp.where(owners[f] == owner, locals_[f], 0)
+        return total
+
+    ask = []
+    for k in range(1, npool):
+        owner = lax.rem(me + k, npool)
+        msg_out[k] = jnp.full((8, 128), slot_at(owner), jnp.int32)
+        ask.append(remote(msg_out.at[k], msg_in.at[k], m_send.at[k], m_recv.at[k], owner))
+        ask[-1].start()
+    h_pair.start()
+    h_other.start()
+
+    @pl.when(a != b)
+    def _():
+        w_far.start()
+
+    arrived[me] = cache[slot_at(me)]
+    answers = []
+    for k in range(1, npool):
+        ask[k - 1].wait_recv()
+        reply[k] = cache[jnp.max(msg_in[k])]
+        answers.append(
+            remote(reply.at[k], arrived.at[me], f_send.at[k], f_recv.at[k], lax.rem(me + npool - k, npool))
+        )
+
+    h_pair.wait_send()
+
+    @pl.when(a == b)
+    def _():
+        w_far.start()
+
+    @pl.when(a != b)
+    def _():
+        w_near.start()
+
+    def h_wait(slot):
+        pltpu.make_async_copy(hid, hbuf.at[rows_at(slot)], h_recv.at[slot]).wait()
+
+    h_wait(pair_slot)
+    h_fwd = remote(hbuf.at[rows_at(pair_slot)], hbuf.at[rows_at(pair_slot)], h_send.at[2], h_recv.at[pair_slot], other)
+    h_fwd.start()
+    w_far.wait_send()
+
+    @pl.when(a != b)
+    def _():
+        w_near.wait_send()
+
+    for k in (4, 3, 5, 2, 6, 1, 7):
+        answers[k - 1].start()
+
+    h_wait(own_slot)
+    h_wait(b * 2 + 1 - x)
+    for s in range(2):
+        pltpu.make_async_copy(wgt, wbuf.at[:, pl.ds(s * HD, HD)], w_recv.at[s]).wait()
+
+    def project(zl):
+        block = jnp.dot(hbuf[rows_at(zl * 2, 2)], wbuf[...], preferred_element_type=jnp.float32)
+        for sx in range(2):
+            for i in range(2):
+                j = zl * 2 + sx
+                src = pbuf.at[j, i]
+                src[...] = block[sx * rows:(sx + 1) * rows, i * HD:(i + 1) * HD].astype(jnp.bfloat16)
+                mine = jnp.logical_and(4 * a + j == me, 2 * b + i == t)
+
+                @pl.when(mine)
+                def _():
+                    pltpu.make_async_copy(src, part.at[x, t], s_recv.at[x, t]).start()
+
+                @pl.when(jnp.logical_not(mine))
+                def _():
+                    remote(src, part.at[x, t], s_send.at[j, i], s_recv.at[x, t], 4 * a + j, 2 * b + i).start()
+
+    project(b)
+    h_wait((1 - b) * 2 + 1 - x)
+    project(1 - b)
+
+    for k in range(1, npool):
+        answers[k - 1].wait_recv()
+    for f in range(fetch):
+        block = arrived[owners[f]]
+        kcat[f * BLK:(f + 1) * BLK] = block[:, 0:HD]
+        vcat[f * BLK:(f + 1) * BLK] = block[:, HD:2 * HD]
+
+    for kind, cat in ((0, kcat), (1, vcat)):
+        total = jnp.zeros((rows, HD), jnp.float32)
+        for s in range(4):
+            pltpu.make_async_copy(pbuf.at[0, 0], part.at[kind, s], s_recv.at[kind, s]).wait()
+            total = total + part[kind, s].astype(jnp.float32)
+        total = total.astype(jnp.bfloat16)
+        cat[fetch * BLK:] = total
+        fresh[:, kind * HD:(kind + 1) * HD] = total
+
+    keys_count = fetch * BLK + rows
+    token = lax.broadcasted_iota(jnp.int32, (rows, BLK), 0)
+    key = lax.broadcasted_iota(jnp.int32, (rows, BLK), 1)
+    scale = float(HD) ** (-0.5)
+
+    @pl.loop(0, q_ref.shape[1] // (2 * HD))
+    def _(step):
+        masks = []
+        for f in range(fetch):
+            allowed = jnp.zeros((rows, BLK), jnp.int32)
+            for r in range(pat.shape[1]):
+                allowed = jnp.where(lax.div(token, RBLK) == r, pat[0, r, f], allowed)
+            masks.append(allowed != 0)
+        masks.append(token >= key)
+        for half in range(2):
+            at = pl.ds(pl.multiple_of(step * 2 * HD + half * HD, HD), HD)
+            raw = rows_by_keys(q_ref[:, at], kcat[...]) * scale
+            scores = [jnp.where(masks[n], raw[:, n * BLK:(n + 1) * BLK], -1e30) for n in range(fetch + 1)]
+            top = scores[0]
+            for n in range(1, fetch + 1):
+                top = jnp.maximum(top, scores[n])
+            top = jnp.max(top, axis=1, keepdims=True)
+            weights = [jnp.exp(s - top) for s in scores]
+            denom = weights[0]
+            for n in range(1, fetch + 1):
+                denom = denom + weights[n]
+            denom = jnp.sum(denom, axis=1, keepdims=True)
+            rounded = jnp.concatenate([w.astype(jnp.bfloat16) for w in weights], axis=1)
+            numer = jnp.dot(rounded, vcat[...], preferred_element_type=jnp.float32)
+            att[:, at] = (numer / denom).astype(jnp.bfloat16)
+
+    h_other.wait_send()
+    h_fwd.wait_send()
+    for k in range(1, npool):
+        ask[k - 1].wait_send()
+        answers[k - 1].wait_send()
+    for j in range(4):
+        for i in range(2):
+            mine = jnp.logical_and(4 * a + j == me, 2 * b + i == t)
+
+            @pl.when(jnp.logical_not(mine))
+            def _():
+                remote(pbuf.at[j, i], part.at[x, t], s_send.at[j, i], s_recv.at[x, t], 4 * a + j, 2 * b + i).wait_send()
+
+
+def fused(hidden_rows, kv_weight, queries, cache_table, retrieval, pattern):
+    rows, depth = hidden_rows.shape
+    cols = kv_weight.shape[1]
+    blocks_dev, _, width = cache_table.shape
+    keys_count = retrieval.shape[1] * BLK + rows
+    dma = pltpu.SemaphoreType.DMA
+    vmem = pl.BlockSpec(memory_space=pltpu.VMEM)
+    smem = pl.BlockSpec(memory_space=pltpu.SMEM)
+    anyw = pl.BlockSpec(memory_space=pl.ANY)
+    bf = jnp.bfloat16
+    return pl.pallas_call(
+        kernel,
+        out_shape=(
+            jax.ShapeDtypeStruct(queries.shape, bf),
+            jax.ShapeDtypeStruct((rows, width), bf),
+        ),
+        in_specs=[anyw, anyw, vmem, vmem, smem, smem],
+        out_specs=(vmem, vmem),
+        scratch_shapes=[
+            pltpu.VMEM((4 * rows, depth), bf),
+            pltpu.VMEM((depth, 2 * cols), bf),
+            pltpu.VMEM((4, 2, rows, HD), bf),
+            pltpu.VMEM((2, 4, rows, HD), bf),
+            pltpu.VMEM((8, 8, 128), jnp.int32),
+            pltpu.VMEM((8, 8, 128), jnp.int32),
+            pltpu.VMEM((8, BLK, width), bf),
+            pltpu.VMEM((8, BLK, width), bf),
+            pltpu.VMEM((keys_count, HD), bf),
+            pltpu.VMEM((keys_count, HD), bf),
+            dma((4,)), dma((3,)), dma((2,)), dma((2,)), dma((8,)), dma((8,)), dma((8,)), dma((8,)),
+            dma((2, 4)), dma((4, 2)),
+        ],
+        compiler_params=pltpu.CompilerParams(
+            collective_id=0, has_side_effects=True, vmem_limit_bytes=32 * 1024 * 1024
+        ),
+        name="blend",
+    )(hidden_rows, kv_weight, queries, cache_table, retrieval, pattern)
+
+
+def fits(mesh, hidden_rows, kv_weight, cache_table, retrieval):
+    return (
+        mesh.shape["pool"] == 8
+        and mesh.shape["tp"] == 4
+        and hidden_rows.shape[0] == 8 * BLK
+        and kv_weight.shape[1] == 8 * HD
+        and cache_table.shape[2] == 8 * HD
+        and retrieval.shape[1] <= 8
+    )
+
+
 def solution(mesh):
     placed = (
         P("pool", "tp"),
@@ -98,10 +350,15 @@
         P("pool", None),
         P("pool", None, None),
     )
-    return jax.shard_map(
-        body,
-        mesh=mesh,
-        in_specs=placed,
-        out_specs=(P("pool", "tp"), P("pool", "tp")),
-        check_vma=False,
-    )
+
+    def run(hidden_rows, kv_weight, queries, cache_table, retrieval, pattern):
+        small = fits(mesh, hidden_rows, kv_weight, cache_table, retrieval)
+        return jax.shard_map(
+            fused if small else body,
+            mesh=mesh,
+            in_specs=placed,
+            out_specs=(P("pool", "tp"), P("pool", "tp")),
+            check_vma=False,
+        )(hidden_rows, kv_weight, queries, cache_table, retrieval, pattern)
+
+    return run

time: 131 us -> 53.9 us (0.41)
  waiting for transfers between devices: 91 us -> 0 us
  Pallas kernels: 0 us -> 46.1 us
  between operations: 14.2 us -> 0.65 us
  starting transfers between devices: 10.8 us -> 0 us
  matrix products: 5.98 us -> 0 us
  other arithmetic: 5.35 us -> 0 us
  local copies, waits for them, and re-layouts: 3.37 us -> 6.73 us
    all_gather x1 -> x0, waiting for transfers between devices: 68.7 us -> none  [body(): lax.all_gather(kv_weight, 'pool', axis=1, tiled=True)]
    pallas_call x0 -> x1, Pallas kernels: none -> 46.1 us  [fused(): pl.pallas_call(kernel, out_shape=(jax.ShapeDtypeStruct(queries.shape, bf)...]
    reduce_scatter x1 -> x0, waiting for transfers between devices: 17.1 us -> none  [body(): lax.psum_scatter(partial_kv.astype(jnp.bfloat16), 'tp', scatter_dimension...]
    all_to_all x2 -> x0, starting transfers between devices: 10.8 us -> none  [the longest x1 7.27 us: body(): lax.all_to_all(request.reshape(npool, 1), 'pool', split_axis=0, concat_ax...]
    unnamed x8 -> x14, local copies, waits for them, and re-layouts: 0.02 us -> 6.73 us
    dot_general x5 -> x0, matrix products: 5.98 us -> none  [the longest x1 3.61 us: body(): jnp.dot(hidden_rows, lax.all_gather(kv_weight, 'pool', axis=1, tiled=True...]
    all_to_all x2 -> x0, waiting for transfers between devices: 4.49 us -> none  [the longest x1 4.49 us: body(): lax.all_to_all(request.reshape(npool, 1), 'pool', split_axis=0, concat_ax...]
    and x2 -> x0, other arithmetic: 1.35 us -> none  [the longest x1 0.69 us: visit(): row_pat = jnp.any(row_blocks & (pat_now[None] != 0), axis=1)]
  transfers between devices with their start and end apart: 4 -> 0, of which waited for: 3 -> 0; matrix products, arithmetic and copies ran while one was open for 9% -> 0% of each run, Pallas kernels for 0% -> 0%
where the time goes in v1:
time: 53.9 us; the launch traced here: 53.5 us
  Pallas kernels  46.1 us (86%)
  local copies, waits for them, and re-layouts  6.73 us (12%)
  between operations  0.65 us (1%)
    pallas_call x1, Pallas kernels, fused(): pl.pallas_call(kernel, out_shape=(jax.ShapeDtypeStruct(queries.shape, bf)...  46.1 us
    unnamed x14, local copies, waits for them, and re-layouts  6.73 us

profile of v1, /device:TPU:0, one launch (start us, length us, event | category | flops | bytes accessed | tf_op | source)
XLA Modules:
  0.0 53.5 jit_solution(18165512336377627844)
XLA Ops:
  0.6 0.0 copy-start
  0.6 1.0 %copy-done = bf16[128,2048]{1,0:T(8,128)(2,1)S(1)} copy-done((bf16[128,2048]{1,0:T(8,128)(2,1)S(1)}, bf16[128,2048]{1,0:T(8,128)(2,1)}, u32[]{:S(2)}) %copy-start) | copy-done | bytes 524312
  1.7 0.0 copy-start.1
  1.7 1.0 %copy-done.1 = bf16[2048,128]{1,0:T(8,128)(2,1)S(1)} copy-done((bf16[2048,128]{1,0:T(8,128)(2,1)S(1)}, bf16[2048,128]{1,0:T(8,128)(2,1)}, u32[]{:S(2)}) %copy-start.1) | copy-done | bytes 524312
  2.7 0.0 copy-start.2
  2.7 1.0 %copy-done.2 = bf16[8,128,256]{2,1,0:T(8,128)(2,1)S(1)} copy-done((bf16[8,128,256]{2,1,0:T(8,128)(2,1)S(1)}, bf16[8,128,256]{2,1,0:T(8,128)(2,1)}, u32[]{:S(2)}) %copy-start.2) | copy-done | bytes 524312
  3.8 0.0 copy-start.3
  3.8 0.9 %copy-done.3 = bf16[128,1024]{1,0:T(8,128)(2,1)S(1)} copy-done((bf16[128,1024]{1,0:T(8,128)(2,1)S(1)}, bf16[128,1024]{1,0:T(8,128)(2,1)}, u32[]{:S(2)}) %copy-start.3) | copy-done | bytes 262168
  4.7 0.0 copy-start.4
  4.7 0.7 %copy-done.4 = s32[1,2,4]{2,1,0:T(2,128)S(1)} copy-done((s32[1,2,4]{2,1,0:T(2,128)S(1)}, s32[1,2,4]{2,1,0:T(2,128)}, u32[]{:S(2)}) %copy-start.4) | copy-done | bytes 56
  5.4 0.0 copy-start.5
  5.4 0.7 %copy-done.5 = s32[1,4]{1,0:T(1,128)S(1)} copy-done((s32[1,4]{1,0:T(1,128)S(1)}, s32[1,4]{1,0:T(1,128)}, u32[]{:S(2)}) %copy-start.5) | copy-done | bytes 40
  6.0 46.1 %blend.1 = (bf16[128,1024]{1,0:T(8,128)(2,1)S(1)}, bf16[128,256]{1,0:T(8,128)(2,1)S(1)}) custom-call(bf16[128,2048]{1,0:T(8,128)(2,1)S(1)} %copy-done, bf16[2048,128]{1,0:T(8,128)(2,1)S(1)} %copy-done.1, bf16[128,1024]{1,0:T(8,128)(2,1)S(1)} %copy-done.3, bf16[8,128,256]{2,1,0:T(8,128)(2,1)S(1)} %copy-done.2, s32[1,4]{1,0:T(1,128)S(1)} %copy-done.5, ...), custom_call_target="tpu_custom_call" | custom-call | tf_op jit(solution)/shard_map/blend/pallas_call | solution.py:304
  52.2 0.7 %copy.10 = bf16[128,1024]{1,0:T(8,128)(2,1)} copy(bf16[128,1024]{1,0:T(8,128)(2,1)S(1)} %get-tuple-element.4) | data formatting | bytes 524288
  52.9 0.6 %copy.11 = bf16[128,256]{1,0:T(8,128)(2,1)} copy(bf16[128,256]{1,0:T(8,128)(2,1)S(1)} %get-tuple-element.5) | data formatting | bytes 131072
Async XLA Ops:
  0.6 1.0 %copy-start = (bf16[128,2048]{1,0:T(8,128)(2,1)S(1)}, bf16[128,2048]{1,0:T(8,128)(2,1)}, u32[]{:S(2)}) copy-start(bf16[128,2048]{1,0:T(8,128)(2,1)} %hid.1) | copy-start | bytes 1572868
  1.7 1.0 %copy-start.1 = (bf16[2048,128]{1,0:T(8,128)(2,1)S(1)}, bf16[2048,128]{1,0:T(8,128)(2,1)}, u32[]{:S(2)}) copy-start(bf16[2048,128]{1,0:T(8,128)(2,1)} %wgt.1) | copy-start | bytes 1572868
  2.7 1.0 %copy-start.2 = (bf16[8,128,256]{2,1,0:T(8,128)(2,1)S(1)}, bf16[8,128,256]{2,1,0:T(8,128)(2,1)}, u32[]{:S(2)}) copy-start(bf16[8,128,256]{2,1,0:T(8,128)(2,1)} %cache.1) | copy-start | bytes 1572868
  3.8 0.9 %copy-start.3 = (bf16[128,1024]{1,0:T(8,128)(2,1)S(1)}, bf16[128,1024]{1,0:T(8,128)(2,1)}, u32[]{:S(2)}) copy-start(bf16[128,1024]{1,0:T(8,128)(2,1)} %q_ref.1) | copy-start | bytes 786436
  4.7 0.7 %copy-start.4 = (s32[1,2,4]{2,1,0:T(2,128)S(1)}, s32[1,2,4]{2,1,0:T(2,128)}, u32[]{:S(2)}) copy-start(s32[1,2,4]{2,1,0:T(2,128)} %pat.1) | copy-start | bytes 100
  5.4 0.7 %copy-start.5 = (s32[1,4]{1,0:T(1,128)S(1)}, s32[1,4]{1,0:T(1,128)}, u32[]{:S(2)}) copy-start(s32[1,4]{1,0:T(1,128)} %retr.1) | copy-start | bytes 52

commit v2 on v1

--- a/solution.py
+++ b/solution.py
@@ -94,13 +94,21 @@
 MESH = pl.DeviceIdType.MESH
 
 
-def kernel(hid, wgt, q_ref, cache, retr, pat, att, fresh, hbuf, wbuf, pbuf, part, msg_out, msg_in,
-           reply, arrived, kcat, vcat, h_recv, h_send, w_recv, w_send, m_recv, m_send, f_recv, f_send,
-           s_recv, s_send):
+def kernel(hid, wgt, q_hbm, cache_hbm, retr_hbm, pat_hbm, att_hbm, fresh_hbm, hbuf, wbuf, pbuf, part,
+           msg_out, msg_in, reply, arrived, kcat, vcat, q_ref, cache, retr, pat, att, fresh,
+           h_recv, p_send, x_send, f_send, w_recv, w_send, v_send, m_recv, m_send, a_recv, a_send,
+           s_recv, s_send, load_sem, out_sem):
     npool = 8
     blocks_dev = cache.shape[0]
     fetch = retr.shape[1]
-    rows = hid.shape[0]
+    rows, depth = hid.shape
+    half_rows, half_depth = rows // 2, depth // 2
+    loads = [
+        pltpu.make_async_copy(src, dst, load_sem.at[n])
+        for n, (src, dst) in enumerate(((retr_hbm, retr), (cache_hbm, cache), (q_hbm, q_ref), (pat_hbm, pat)))
+    ]
+    for load in loads:
+        load.start()
     me = lax.axis_index("pool")
     t = lax.axis_index("tp")
     z, x = lax.div(me, 2), lax.rem(me, 2)
@@ -110,6 +118,11 @@
     other = z * 2 + 1 - x
     far = (2 - a) * 2 + x
 
+    def peer(k):
+        pa = 1 - a if k & 4 else a
+        pb = 1 - b if k & 2 else b
+        return (2 * pa + pb) * 2 + (1 - x if k & 1 else x)
+
     def remote(src, dst, ssem, rsem, pool, tp=None):
         where = {"pool": pool} if tp is None else {"pool": pool, "tp": tp}
         return pltpu.make_async_remote_copy(
@@ -119,34 +132,59 @@
     def rows_at(slot, count=1):
         return pl.ds(pl.multiple_of(slot * rows, rows), count * rows)
 
+    def half_at(slot, c):
+        return pl.ds(pl.multiple_of(slot * rows + c * half_rows, half_rows), half_rows)
+
     def cols_at(slot):
         return pl.ds(pl.multiple_of(slot * HD, HD), HD)
 
     own_slot = b * 2 + x
     pair_slot = (1 - b) * 2 + x
-    own_h = pltpu.make_async_copy(hid, hbuf.at[rows_at(own_slot)], h_recv.at[own_slot])
-    own_h.start()
-
-    @pl.when(a == b)
-    def _():
-        pltpu.make_async_copy(wgt, wbuf.at[:, cols_at(b)], w_recv.at[b]).start()
+    halves = (0, 1)
+    h_part = [hid.at[pl.ds(c * half_rows, half_rows)] for c in halves]
+    w_part = [wgt.at[pl.ds(c * half_depth, half_depth)] for c in halves]
+    w_land = [wbuf.at[pl.ds(c * half_depth, half_depth), cols_at(b)] for c in halves]
 
     barrier = pltpu.get_barrier_semaphore()
     for k in range(1, npool):
-        pl.semaphore_signal(barrier, inc=1, device_id={"pool": lax.rem(me + k, npool)}, device_id_type=MESH)
+        pl.semaphore_signal(barrier, inc=1, device_id={"pool": peer(k)}, device_id_type=MESH)
     for sx in range(2):
         for k in range(1, 4):
             pl.semaphore_signal(
                 barrier, inc=1,
                 device_id={"pool": (2 * a + y) * 2 + sx, "tp": lax.rem(t + k, 4)}, device_id_type=MESH,
             )
+    own_h = [pltpu.make_async_copy(h_part[c], hbuf.at[half_at(own_slot, c)], h_recv.at[own_slot, c]) for c in halves]
+    for c in halves:
+        own_h[c].start()
+
+    @pl.when(a == b)
+    def _():
+        for c in halves:
+            pltpu.make_async_copy(w_part[c], w_land[c], w_recv.at[b, c]).start()
+
     pl.semaphore_wait(barrier, npool - 1 + jnp.where(y == b, 4, 8))
 
-    h_pair = remote(hid, hbuf.at[rows_at(own_slot)], h_send.at[0], h_recv.at[own_slot], pair)
-    h_other = remote(hid, hbuf.at[rows_at(own_slot)], h_send.at[1], h_recv.at[own_slot], other)
-    w_far = remote(wgt, wbuf.at[:, cols_at(b)], w_send.at[0], w_recv.at[b], far)
-    w_near = remote(wgt, wbuf.at[:, cols_at(b)], w_send.at[1], w_recv.at[b], pair)
-
+    h_pair = [remote(h_part[c], hbuf.at[half_at(own_slot, c)], p_send.at[c], h_recv.at[own_slot, c], pair) for c in halves]
+    h_other = [remote(h_part[c], hbuf.at[half_at(own_slot, c)], x_send.at[c], h_recv.at[own_slot, c], other) for c in halves]
+    h_fwd = [
+        remote(hbuf.at[half_at(pair_slot, c)], hbuf.at[half_at(pair_slot, c)], f_send.at[c], h_recv.at[pair_slot, c], other)
+        for c in halves
+    ]
+    w_far = [remote(w_part[c], w_land[c], w_send.at[c], w_recv.at[b, c], far) for c in halves]
+    w_near = [remote(w_part[c], w_land[c], v_send.at[c], w_recv.at[b, c], pair) for c in halves]
+
+    for c in halves:
+        h_pair[c].start()
+    for c in halves:
+        h_other[c].start()
+
+    @pl.when(a != b)
+    def _():
+        for c in halves:
+            w_far[c].start()
+
+    loads[0].wait()
     wanted = [retr[0, f] for f in range(fetch)]
     owners = [lax.div(v, blocks_dev) for v in wanted]
     locals_ = [lax.rem(v, blocks_dev) for v in wanted]
@@ -157,57 +195,49 @@
             total = total + jnp.where(owners[f] == owner, locals_[f], 0)
         return total
 
-    ask = []
+    ask, answers = [None], [None]
     for k in range(1, npool):
-        owner = lax.rem(me + k, npool)
-        msg_out[k] = jnp.full((8, 128), slot_at(owner), jnp.int32)
-        ask.append(remote(msg_out.at[k], msg_in.at[k], m_send.at[k], m_recv.at[k], owner))
-        ask[-1].start()
-    h_pair.start()
-    h_other.start()
-
-    @pl.when(a != b)
-    def _():
-        w_far.start()
-
+        msg_out[k] = jnp.full((8, 128), slot_at(peer(k)), jnp.int32)
+        ask.append(remote(msg_out.at[k], msg_in.at[k], m_send.at[k], m_recv.at[k], peer(k)))
+        ask[k].start()
+    loads[1].wait()
     arrived[me] = cache[slot_at(me)]
-    answers = []
     for k in range(1, npool):
-        ask[k - 1].wait_recv()
+        ask[k].wait_recv()
         reply[k] = cache[jnp.max(msg_in[k])]
-        answers.append(
-            remote(reply.at[k], arrived.at[me], f_send.at[k], f_recv.at[k], lax.rem(me + npool - k, npool))
-        )
-
-    h_pair.wait_send()
-
-    @pl.when(a == b)
-    def _():
-        w_far.start()
-
-    @pl.when(a != b)
-    def _():
-        w_near.start()
-
-    def h_wait(slot):
-        pltpu.make_async_copy(hid, hbuf.at[rows_at(slot)], h_recv.at[slot]).wait()
-
-    h_wait(pair_slot)
-    h_fwd = remote(hbuf.at[rows_at(pair_slot)], hbuf.at[rows_at(pair_slot)], h_send.at[2], h_recv.at[pair_slot], other)
-    h_fwd.start()
-    w_far.wait_send()
-
-    @pl.when(a != b)
-    def _():
-        w_near.wait_send()
-
-    for k in (4, 3, 5, 2, 6, 1, 7):
-        answers[k - 1].start()
-
-    h_wait(own_slot)
-    h_wait(b * 2 + 1 - x)
-    for s in range(2):
-        pltpu.make_async_copy(wgt, wbuf.at[:, pl.ds(s * HD, HD)], w_recv.at[s]).wait()
+        answers.append(remote(reply.at[k], arrived.at[me], a_send.at[k], a_recv.at[k], peer(k)))
+
+    def h_wait(slot, c):
+        pltpu.make_async_copy(h_part[c], hbuf.at[half_at(slot, c)], h_recv.at[slot, c]).wait()
+
+    for c in halves:
+        h_pair[c].wait_send()
+
+        @pl.when(a == b)
+        def _():
+            w_far[c].start()
+
+        @pl.when(a != b)
+        def _():
+            w_near[c].start()
+
+        h_wait(pair_slot, c)
+        h_fwd[c].start()
+    for c in halves:
+        w_far[c].wait_send()
+
+        @pl.when(a != b)
+        def _():
+            w_near[c].wait_send()
+
+        for k in ((6, 7, 4, 5), (2, 3, 1))[c]:
+            answers[k].start()
+
+    for c in halves:
+        h_wait(own_slot, c)
+        h_wait(b * 2 + 1 - x, c)
+        for s in range(2):
+            pltpu.make_async_copy(w_part[c], wbuf.at[pl.ds(c * half_depth, half_depth), pl.ds(s * HD, HD)], w_recv.at[s, c]).wait()
 
     def project(zl):
         block = jnp.dot(hbuf[rows_at(zl * 2, 2)], wbuf[...], preferred_element_type=jnp.float32)
@@ -227,11 +257,12 @@
                     remote(src, part.at[x, t], s_send.at[j, i], s_recv.at[x, t], 4 * a + j, 2 * b + i).start()
 
     project(b)
-    h_wait((1 - b) * 2 + 1 - x)
+    for c in halves:
+        h_wait((1 - b) * 2 + 1 - x, c)
     project(1 - b)
 
     for k in range(1, npool):
-        answers[k - 1].wait_recv()
+        answers[k].wait_recv()
     for f in range(fetch):
         block = arrived[owners[f]]
         kcat[f * BLK:(f + 1) * BLK] = block[:, 0:HD]
@@ -245,6 +276,10 @@
         total = total.astype(jnp.bfloat16)
         cat[fetch * BLK:] = total
         fresh[:, kind * HD:(kind + 1) * HD] = total
+    fresh_out = pltpu.make_async_copy(fresh, fresh_hbm, out_sem.at[0])
+    fresh_out.start()
+    loads[2].wait()
+    loads[3].wait()
 
     keys_count = fetch * BLK + rows
     token = lax.broadcasted_iota(jnp.int32, (rows, BLK), 0)
@@ -276,12 +311,19 @@
             rounded = jnp.concatenate([w.astype(jnp.bfloat16) for w in weights], axis=1)
             numer = jnp.dot(rounded, vcat[...], preferred_element_type=jnp.float32)
             att[:, at] = (numer / denom).astype(jnp.bfloat16)
-
-    h_other.wait_send()
-    h_fwd.wait_send()
+        at = pl.ds(pl.multiple_of(step * 2 * HD, 2 * HD), 2 * HD)
+        pltpu.make_async_copy(att.at[:, at], att_hbm.at[:, at], out_sem.at[1 + step]).start()
+
+    for c in halves:
+        h_other[c].wait_send()
+        h_fwd[c].wait_send()
     for k in range(1, npool):
-        ask[k - 1].wait_send()
-        answers[k - 1].wait_send()
+        ask[k].wait_send()
+        answers[k].wait_send()
+    fresh_out.wait()
+    for n in range(4):
+        at = pl.ds(n * 2 * HD, 2 * HD)
+        pltpu.make_async_copy(att.at[:, at], att_hbm.at[:, at], out_sem.at[1 + n]).wait()
     for j in range(4):
         for i in range(2):
             mine = jnp.logical_and(4 * a + j == me, 2 * b + i == t)
@@ -297,8 +339,6 @@
     blocks_dev, _, width = cache_table.shape
     keys_count = retrieval.shape[1] * BLK + rows
     dma = pltpu.SemaphoreType.DMA
-    vmem = pl.BlockSpec(memory_space=pltpu.VMEM)
-    smem = pl.BlockSpec(memory_space=pltpu.SMEM)
     anyw = pl.BlockSpec(memory_space=pl.ANY)
     bf = jnp.bfloat16
     return pl.pallas_call(
@@ -307,8 +347,8 @@
             jax.ShapeDtypeStruct(queries.shape, bf),
             jax.ShapeDtypeStruct((rows, width), bf),
         ),
-        in_specs=[anyw, anyw, vmem, vmem, smem, smem],
-        out_specs=(vmem, vmem),
+        in_specs=[anyw] * 6,
+        out_specs=(anyw, anyw),
         scratch_shapes=[
             pltpu.VMEM((4 * rows, depth), bf),
             pltpu.VMEM((depth, 2 * cols), bf),
@@ -320,11 +360,17 @@
             pltpu.VMEM((8, BLK, width), bf),
             pltpu.VMEM((keys_count, HD), bf),
             pltpu.VMEM((keys_count, HD), bf),
-            dma((4,)), dma((3,)), dma((2,)), dma((2,)), dma((8,)), dma((8,)), dma((8,)), dma((8,)),
-            dma((2, 4)), dma((4, 2)),
+            pltpu.VMEM(queries.shape, bf),
+            pltpu.VMEM(cache_table.shape, bf),
+            pltpu.SMEM(retrieval.shape, jnp.int32),
+            pltpu.SMEM(pattern.shape, jnp.int32),
+            pltpu.VMEM(queries.shape, bf),
+            pltpu.VMEM((rows, width), bf),
+            dma((4, 2)), dma((2,)), dma((2,)), dma((2,)), dma((2, 2)), dma((2,)), dma((2,)),
+            dma((8,)), dma((8,)), dma((8,)), dma((8,)), dma((2, 4)), dma((4, 2)), dma((4,)), dma((5,)),
         ],
         compiler_params=pltpu.CompilerParams(
-            collective_id=0, has_side_effects=True, vmem_limit_bytes=32 * 1024 * 1024
+            collective_id=0, has_side_effects=True, vmem_limit_bytes=60 * 1024 * 1024
         ),
         name="blend",
     )(hidden_rows, kv_weight, queries, cache_table, retrieval, pattern)

time: 53.9 us -> 54.1 us (level)
  Pallas kernels: 46.1 us -> 50.9 us
  local copies, waits for them, and re-layouts: 6.73 us -> 2.33 us
    pallas_call x1, Pallas kernels: 46.1 us -> 50.9 us  [fused(): pl.pallas_call(kernel, out_shape=(jax.ShapeDtypeStruct(queries.shape, bf)...]
    unnamed x14 -> x4, local copies, waits for them, and re-layouts: 6.73 us -> 2.33 us
where the time goes in v2:
time: 54.1 us; the launch traced here: 53.9 us
  Pallas kernels  50.9 us (94%)
  local copies, waits for them, and re-layouts  2.33 us (4%)
  between operations  0.65 us (1%)
    pallas_call x1, Pallas kernels, fused(): pl.pallas_call(kernel, out_shape=(jax.ShapeDtypeStruct(queries.shape, bf)...  50.9 us
    unnamed x4, local copies, waits for them, and re-layouts  2.33 us

profile of v2, /device:TPU:0, one launch (start us, length us, event | category | flops | bytes accessed | tf_op | source)
XLA Modules:
  0.0 53.9 jit_solution(9648609268924454891)
XLA Ops:
  0.6 50.9 %blend.1 = (bf16[128,1024]{1,0:T(8,128)(2,1)}, bf16[128,256]{1,0:T(8,128)(2,1)}) custom-call(bf16[128,2048]{1,0:T(8,128)(2,1)} %hid.1, bf16[2048,128]{1,0:T(8,128)(2,1)} %wgt.1, bf16[128,1024]{1,0:T(8,128)(2,1)} %q_hbm.1, bf16[8,128,256]{2,1,0:T(8,128)(2,1)} %cache_hbm.1, s32[1,4]{1,0:T(1,128)} %retr_hbm.1, s32[1,2,4]{2,1,0:T(2,128)} %pat_hbm.1), custom_call_target="tpu_custom_call" | custom-call | tf_op jit(solution)/shard_map/blend/pallas_call | solution.py:344
  51.6 0.0 copy-start
  51.6 1.7 %copy.10 = bf16[128,1024]{1,0:T(8,128)(2,1)} copy(bf16[128,1024]{1,0:T(8,128)(2,1)} %get-tuple-element.4) | data formatting | bytes 524288
  53.3 0.0 copy-done
  53.3 0.6 %copy.11 = bf16[128,256]{1,0:T(8,128)(2,1)} copy(bf16[128,256]{1,0:T(8,128)(2,1)S(1)} %copy-done) | data formatting | bytes 131072
Async XLA Ops:
  51.6 1.7 %copy-start = (bf16[128,256]{1,0:T(8,128)(2,1)S(1)}, bf16[128,256]{1,0:T(8,128)(2,1)}, u32[]{:S(2)}) copy-start(bf16[128,256]{1,0:T(8,128)(2,1)} %get-tuple-element.5) | copy-start | bytes 196612

commit v3 on v2

--- a/solution.py
+++ b/solution.py
@@ -94,10 +94,10 @@
 MESH = pl.DeviceIdType.MESH
 
 
-def kernel(hid, wgt, q_hbm, cache_hbm, retr_hbm, pat_hbm, att_hbm, fresh_hbm, hbuf, wbuf, pbuf, part,
-           msg_out, msg_in, reply, arrived, kcat, vcat, q_ref, cache, retr, pat, att, fresh,
+def kernel(hid, wgt, q_hbm, cache_hbm, retr_hbm, pat_hbm, att, fresh, hbuf, wbuf, wsrc, pbuf, part,
+           msg_out, msg_in, reply, arrived, kcat, vcat, q_ref, cache, retr, pat,
            h_recv, p_send, x_send, f_send, w_recv, w_send, v_send, m_recv, m_send, a_recv, a_send,
-           s_recv, s_send, load_sem, out_sem):
+           s_recv, s_send, load_sem):
     npool = 8
     blocks_dev = cache.shape[0]
     fetch = retr.shape[1]
@@ -105,10 +105,10 @@
     half_rows, half_depth = rows // 2, depth // 2
     loads = [
         pltpu.make_async_copy(src, dst, load_sem.at[n])
-        for n, (src, dst) in enumerate(((retr_hbm, retr), (cache_hbm, cache), (q_hbm, q_ref), (pat_hbm, pat)))
+        for n, (src, dst) in enumerate(((retr_hbm, retr), (cache_hbm, cache), (q_hbm, q_ref), (pat_hbm, pat), (wgt, wsrc)))
     ]
-    for load in loads:
-        load.start()
+    loads[0].start()
+    loads[4].start()
     me = lax.axis_index("pool")
     t = lax.axis_index("tp")
     z, x = lax.div(me, 2), lax.rem(me, 2)
@@ -141,10 +141,23 @@
     own_slot = b * 2 + x
     pair_slot = (1 - b) * 2 + x
     halves = (0, 1)
-    h_part = [hid.at[pl.ds(c * half_rows, half_rows)] for c in halves]
-    w_part = [wgt.at[pl.ds(c * half_depth, half_depth)] for c in halves]
+    h_in = [hid.at[pl.ds(c * half_rows, half_rows)] for c in halves]
+    w_in = [wgt.at[pl.ds(c * half_depth, half_depth)] for c in halves]
+    h_part = [hbuf.at[half_at(own_slot, c)] for c in halves]
+    w_part = [wsrc.at[pl.ds(c * half_depth, half_depth)] for c in halves]
     w_land = [wbuf.at[pl.ds(c * half_depth, half_depth), cols_at(b)] for c in halves]
 
+    own_h = [pltpu.make_async_copy(h_in[c], hbuf.at[half_at(own_slot, c)], h_recv.at[own_slot, c]) for c in halves]
+    for c in halves:
+        own_h[c].start()
+
+    @pl.when(a == b)
+    def _():
+        for c in halves:
+            pltpu.make_async_copy(w_in[c], w_land[c], w_recv.at[b, c]).start()
+
+    for n in (1, 3, 2):
+        loads[n].start()
     barrier = pltpu.get_barrier_semaphore()
     for k in range(1, npool):
         pl.semaphore_signal(barrier, inc=1, device_id={"pool": peer(k)}, device_id_type=MESH)
@@ -154,15 +167,10 @@
                 barrier, inc=1,
                 device_id={"pool": (2 * a + y) * 2 + sx, "tp": lax.rem(t + k, 4)}, device_id_type=MESH,
             )
-    own_h = [pltpu.make_async_copy(h_part[c], hbuf.at[half_at(own_slot, c)], h_recv.at[own_slot, c]) for c in halves]
-    for c in halves:
-        own_h[c].start()
-
-    @pl.when(a == b)
-    def _():
-        for c in halves:
-            pltpu.make_async_copy(w_part[c], w_land[c], w_recv.at[b, c]).start()
-
+    for c in halves:
+        own_h[c].wait()
+    loads[4].wait()
+    loads[0].wait()
     pl.semaphore_wait(barrier, npool - 1 + jnp.where(y == b, 4, 8))
 
     h_pair = [remote(h_part[c], hbuf.at[half_at(own_slot, c)], p_send.at[c], h_recv.at[own_slot, c], pair) for c in halves]
@@ -184,7 +192,6 @@
         for c in halves:
             w_far[c].start()
 
-    loads[0].wait()
     wanted = [retr[0, f] for f in range(fetch)]
     owners = [lax.div(v, blocks_dev) for v in wanted]
     locals_ = [lax.rem(v, blocks_dev) for v in wanted]
@@ -208,7 +215,7 @@
         answers.append(remote(reply.at[k], arrived.at[me], a_send.at[k], a_recv.at[k], peer(k)))
 
     def h_wait(slot, c):
-        pltpu.make_async_copy(h_part[c], hbuf.at[half_at(slot, c)], h_recv.at[slot, c]).wait()
+        pltpu.make_async_copy(h_in[c], hbuf.at[half_at(slot, c)], h_recv.at[slot, c]).wait()
 
     for c in halves:
         h_pair[c].wait_send()
@@ -234,7 +241,6 @@
             answers[k].start()
 
     for c in halves:
-        h_wait(own_slot, c)
         h_wait(b * 2 + 1 - x, c)
         for s in range(2):
             pltpu.make_async_copy(w_part[c], wbuf.at[pl.ds(c * half_depth, half_depth), pl.ds(s * HD, HD)], w_recv.at[s, c]).wait()
@@ -276,8 +282,6 @@
         total = total.astype(jnp.bfloat16)
         cat[fetch * BLK:] = total
         fresh[:, kind * HD:(kind + 1) * HD] = total
-    fresh_out = pltpu.make_async_copy(fresh, fresh_hbm, out_sem.at[0])
-    fresh_out.start()
     loads[2].wait()
     loads[3].wait()
 
@@ -311,8 +315,6 @@
             rounded = jnp.concatenate([w.astype(jnp.bfloat16) for w in weights], axis=1)
             numer = jnp.dot(rounded, vcat[...], preferred_element_type=jnp.float32)
             att[:, at] = (numer / denom).astype(jnp.bfloat16)
-        at = pl.ds(pl.multiple_of(step * 2 * HD, 2 * HD), 2 * HD)
-        pltpu.make_async_copy(att.at[:, at], att_hbm.at[:, at], out_sem.at[1 + step]).start()
 
     for c in halves:
         h_other[c].wait_send()
@@ -320,10 +322,6 @@
     for k in range(1, npool):
         ask[k].wait_send()
         answers[k].wait_send()
-    fresh_out.wait()
-    for n in range(4):
-        at = pl.ds(n * 2 * HD, 2 * HD)
-        pltpu.make_async_copy(att.at[:, at], att_hbm.at[:, at], out_sem.at[1 + n]).wait()
     for j in range(4):
         for i in range(2):
             mine = jnp.logical_and(4 * a + j == me, 2 * b + i == t)
@@ -339,19 +337,21 @@
     blocks_dev, _, width = cache_table.shape
     keys_count = retrieval.shape[1] * BLK + rows
     dma = pltpu.SemaphoreType.DMA
-    anyw = pl.BlockSpec(memory_space=pl.ANY)
+    hbm = pl.BlockSpec(memory_space=pltpu.HBM)
+    vmem = pl.BlockSpec(memory_space=pltpu.VMEM)
     bf = jnp.bfloat16
     return pl.pallas_call(
         kernel,
         out_shape=(
-            jax.ShapeDtypeStruct(queries.shape, bf),
-            jax.ShapeDtypeStruct((rows, width), bf),
+            pltpu.VMEM(queries.shape, bf),
+            pltpu.VMEM((rows, width), bf),
         ),
-        in_specs=[anyw] * 6,
-        out_specs=(anyw, anyw),
+        in_specs=[hbm] * 6,
+        out_specs=(vmem, vmem),
         scratch_shapes=[
             pltpu.VMEM((4 * rows, depth), bf),
             pltpu.VMEM((depth, 2 * cols), bf),
+            pltpu.VMEM((depth, cols), bf),
             pltpu.VMEM((4, 2, rows, HD), bf),
             pltpu.VMEM((2, 4, rows, HD), bf),
             pltpu.VMEM((8, 8, 128), jnp.int32),
@@ -364,13 +364,11 @@
             pltpu.VMEM(cache_table.shape, bf),
             pltpu.SMEM(retrieval.shape, jnp.int32),
             pltpu.SMEM(pattern.shape, jnp.int32),
-            pltpu.VMEM(queries.shape, bf),
-            pltpu.VMEM((rows, width), bf),
             dma((4, 2)), dma((2,)), dma((2,)), dma((2,)), dma((2, 2)), dma((2,)), dma((2,)),
-            dma((8,)), dma((8,)), dma((8,)), dma((8,)), dma((2, 4)), dma((4, 2)), dma((4,)), dma((5,)),
+            dma((8,)), dma((8,)), dma((8,)), dma((8,)), dma((2, 4)), dma((4, 2)), dma((5,)),
         ],
         compiler_params=pltpu.CompilerParams(
-            collective_id=0, has_side_effects=True, vmem_limit_bytes=60 * 1024 * 1024
+            collective_id=0, has_side_effects=True, vmem_limit_bytes=62 * 1024 * 1024
         ),
         name="blend",
     )(hidden_rows, kv_weight, queries, cache_table, retrieval, pattern)

time: 54.1 us -> 52 us (0.961)
  Pallas kernels: 50.9 us -> 49.9 us
  local copies, waits for them, and re-layouts: 2.33 us -> 1.33 us
    pallas_call x1, Pallas kernels: 50.9 us -> 49.9 us  [fused(): pl.pallas_call(kernel, out_shape=(pltpu.VMEM(queries.shape, bf), pltpu.VM...]
    unnamed x4 -> x2, local copies, waits for them, and re-layouts: 2.33 us -> 1.33 us
where the time goes in v3:
time: 52 us; the launch traced here: 51.9 us
  Pallas kernels  49.9 us (96%)
  local copies, waits for them, and re-layouts  1.33 us (3%)
  between operations  0.64 us (1%)
    pallas_call x1, Pallas kernels, fused(): pl.pallas_call(kernel, out_shape=(pltpu.VMEM(queries.shape, bf), pltpu.VM...  49.9 us
    unnamed x2, local copies, waits for them, and re-layouts  1.33 us

profile of v3, /device:TPU:0, one launch (start us, length us, event | category | flops | bytes accessed | tf_op | source)
XLA Modules:
  0.0 51.9 jit_solution(16719377701458104035)
XLA Ops:
  0.6 49.9 %blend.1 = (bf16[128,1024]{1,0:T(8,128)(2,1)S(1)}, bf16[128,256]{1,0:T(8,128)(2,1)S(1)}) custom-call(bf16[128,2048]{1,0:T(8,128)(2,1)} %hid.1, bf16[2048,128]{1,0:T(8,128)(2,1)} %wgt.1, bf16[128,1024]{1,0:T(8,128)(2,1)} %q_hbm.1, bf16[8,128,256]{2,1,0:T(8,128)(2,1)} %cache_hbm.1, s32[1,4]{1,0:T(1,128)} %retr_hbm.1, s32[1,2,4]{2,1,0:T(2,128)} %pat_hbm.1), custom_call_target="tpu_custom_call" | custom-call | tf_op jit(solution)/shard_map/blend/pallas_call | solution.py:343
  50.5 0.7 %copy.10 = bf16[128,1024]{1,0:T(8,128)(2,1)} copy(bf16[128,1024]{1,0:T(8,128)(2,1)S(1)} %get-tuple-element.2) | data formatting | bytes 524288
  51.2 0.6 %copy.11 = bf16[128,256]{1,0:T(8,128)(2,1)} copy(bf16[128,256]{1,0:T(8,128)(2,1)S(1)} %get-tuple-element.3) | data formatting | bytes 131072

commit v4 on v3

--- a/solution.py
+++ b/solution.py
@@ -95,7 +95,7 @@
 
 
 def kernel(hid, wgt, q_hbm, cache_hbm, retr_hbm, pat_hbm, att, fresh, hbuf, wbuf, wsrc, pbuf, part,
-           msg_out, msg_in, reply, arrived, kcat, vcat, q_ref, cache, retr, pat,
+           msg_out, msg_in, reply, arrived, top_ref, sum_ref, acc_ref, q_ref, cache, retr, pat,
            h_recv, p_send, x_send, f_send, w_recv, w_send, v_send, m_recv, m_send, a_recv, a_send,
            s_recv, s_send, load_sem):
     npool = 8
@@ -208,11 +208,11 @@
         ask.append(remote(msg_out.at[k], msg_in.at[k], m_send.at[k], m_recv.at[k], peer(k)))
         ask[k].start()
     loads[1].wait()
-    arrived[me] = cache[slot_at(me)]
+    arrived[0] = cache[slot_at(me)]
     for k in range(1, npool):
         ask[k].wait_recv()
         reply[k] = cache[jnp.max(msg_in[k])]
-        answers.append(remote(reply.at[k], arrived.at[me], a_send.at[k], a_recv.at[k], peer(k)))
+        answers.append(remote(reply.at[k], arrived.at[k], a_send.at[k], a_recv.at[k], peer(k)))
 
     def h_wait(slot, c):
         pltpu.make_async_copy(h_in[c], hbuf.at[half_at(slot, c)], h_recv.at[slot, c]).wait()
@@ -237,7 +237,7 @@
         def _():
             w_near[c].wait_send()
 
-        for k in ((6, 7, 4, 5), (2, 3, 1))[c]:
+        for k in ((6, 7), (2, 3, 1))[c]:
             answers[k].start()
 
     for c in halves:
@@ -267,61 +267,85 @@
         h_wait((1 - b) * 2 + 1 - x, c)
     project(1 - b)
 
-    for k in range(1, npool):
-        answers[k].wait_recv()
-    for f in range(fetch):
-        block = arrived[owners[f]]
-        kcat[f * BLK:(f + 1) * BLK] = block[:, 0:HD]
-        vcat[f * BLK:(f + 1) * BLK] = block[:, HD:2 * HD]
-
-    for kind, cat in ((0, kcat), (1, vcat)):
+    for k, first in ((4, 6), (5, 7)):
+        answers[first].wait_send()
+        answers[k].start()
+
+    for kind in range(2):
         total = jnp.zeros((rows, HD), jnp.float32)
-        for s in range(4):
-            pltpu.make_async_copy(pbuf.at[0, 0], part.at[kind, s], s_recv.at[kind, s]).wait()
-            total = total + part[kind, s].astype(jnp.float32)
-        total = total.astype(jnp.bfloat16)
-        cat[fetch * BLK:] = total
-        fresh[:, kind * HD:(kind + 1) * HD] = total
+        for n in range(4):
+            pltpu.make_async_copy(pbuf.at[0, 0], part.at[kind, n], s_recv.at[kind, n]).wait()
+            total = total + part[kind, n].astype(jnp.float32)
+        fresh[:, kind * HD:(kind + 1) * HD] = total.astype(jnp.bfloat16)
     loads[2].wait()
     loads[3].wait()
 
-    keys_count = fetch * BLK + rows
-    token = lax.broadcasted_iota(jnp.int32, (rows, BLK), 0)
-    key = lax.broadcasted_iota(jnp.int32, (rows, BLK), 1)
     scale = float(HD) ** (-0.5)
 
-    @pl.loop(0, q_ref.shape[1] // (2 * HD))
-    def _(step):
-        masks = []
-        for f in range(fetch):
-            allowed = jnp.zeros((rows, BLK), jnp.int32)
-            for r in range(pat.shape[1]):
-                allowed = jnp.where(lax.div(token, RBLK) == r, pat[0, r, f], allowed)
-            masks.append(allowed != 0)
-        masks.append(token >= key)
-        for half in range(2):
-            at = pl.ds(pl.multiple_of(step * 2 * HD + half * HD, HD), HD)
-            raw = rows_by_keys(q_ref[:, at], kcat[...]) * scale
-            scores = [jnp.where(masks[n], raw[:, n * BLK:(n + 1) * BLK], -1e30) for n in range(fetch + 1)]
+    def allowed(k):
+        owner = me if k == 0 else peer(k)
+        token = lax.broadcasted_iota(jnp.int32, (rows, BLK), 0)
+        mask = jnp.zeros((rows, BLK), jnp.int32)
+        for r in range(pat.shape[1]):
+            named = jnp.int32(0)
+            for f in range(fetch):
+                named = named + jnp.where(owners[f] == owner, pat[0, r, f], 0)
+            mask = jnp.where(lax.div(token, RBLK) == r, named, mask)
+        return mask != 0
+
+    def stage(near, ks, last):
+        @pl.loop(0, q_ref.shape[1] // HD, unroll=2)
+        def _(head):
+            at = pl.ds(pl.multiple_of(head * HD, HD), HD)
+            masks = [allowed(k) for k in ks]
+            keys = [arrived[k, :, 0:HD] for k in ks]
+            vals = [arrived[k, :, HD:2 * HD] for k in ks]
+            if near:
+                token = lax.broadcasted_iota(jnp.int32, (rows, rows), 0)
+                masks.append(token >= lax.broadcasted_iota(jnp.int32, (rows, rows), 1))
+                keys.append(fresh[:, 0:HD])
+                vals.append(fresh[:, HD:2 * HD])
+            raw = rows_by_keys(q_ref[:, at], jnp.concatenate(keys, axis=0)) * scale
+            scores = [jnp.where(m, raw[:, n * BLK:(n + 1) * BLK], -1e30) for n, m in enumerate(masks)]
             top = scores[0]
-            for n in range(1, fetch + 1):
-                top = jnp.maximum(top, scores[n])
+            for one in scores[1:]:
+                top = jnp.maximum(top, one)
             top = jnp.max(top, axis=1, keepdims=True)
-            weights = [jnp.exp(s - top) for s in scores]
+            if not near:
+                before = top_ref[head]
+                top = jnp.maximum(before, top)
+                factor = jnp.exp(before - top)
+            else:
+                top = jnp.broadcast_to(top, (rows, HD))
+            weights = [jnp.exp(one - top) for one in scores]
             denom = weights[0]
-            for n in range(1, fetch + 1):
-                denom = denom + weights[n]
-            denom = jnp.sum(denom, axis=1, keepdims=True)
+            for one in weights[1:]:
+                denom = denom + one
             rounded = jnp.concatenate([w.astype(jnp.bfloat16) for w in weights], axis=1)
-            numer = jnp.dot(rounded, vcat[...], preferred_element_type=jnp.float32)
-            att[:, at] = (numer / denom).astype(jnp.bfloat16)
+            numer = jnp.dot(rounded, jnp.concatenate(vals, axis=0), preferred_element_type=jnp.float32)
+            if not near:
+                denom = denom + factor * sum_ref[head]
+                numer = numer + factor * acc_ref[head]
+            if last:
+                att[:, at] = (numer / jnp.sum(denom, axis=1, keepdims=True)).astype(jnp.bfloat16)
+            else:
+                top_ref[head] = top
+                sum_ref[head] = denom
+                acc_ref[head] = numer
+
+    for near, ks, last in ((True, (0, 1, 2, 3), False), (False, (6, 7), False), (False, (4, 5), True)):
+        for k in ks:
+            if k:
+                answers[k].wait_recv()
+        stage(near, ks, last)
 
     for c in halves:
         h_other[c].wait_send()
         h_fwd[c].wait_send()
     for k in range(1, npool):
         ask[k].wait_send()
-        answers[k].wait_send()
+        if k not in (6, 7):
+            answers[k].wait_send()
     for j in range(4):
         for i in range(2):
             mine = jnp.logical_and(4 * a + j == me, 2 * b + i == t)
@@ -335,7 +359,6 @@
     rows, depth = hidden_rows.shape
     cols = kv_weight.shape[1]
     blocks_dev, _, width = cache_table.shape
-    keys_count = retrieval.shape[1] * BLK + rows
     dma = pltpu.SemaphoreType.DMA
     hbm = pl.BlockSpec(memory_space=pltpu.HBM)
     vmem = pl.BlockSpec(memory_space=pltpu.VMEM)
@@ -358,8 +381,9 @@
             pltpu.VMEM((8, 8, 128), jnp.int32),
             pltpu.VMEM((8, BLK, width), bf),
             pltpu.VMEM((8, BLK, width), bf),
-            pltpu.VMEM((keys_count, HD), bf),
-            pltpu.VMEM((keys_count, HD), bf),
+            pltpu.VMEM((queries.shape[1] // HD, rows, HD), jnp.float32),
+            pltpu.VMEM((queries.shape[1] // HD, rows, HD), jnp.float32),
+            pltpu.VMEM((queries.shape[1] // HD, rows, HD), jnp.float32),
             pltpu.VMEM(queries.shape, bf),
             pltpu.VMEM(cache_table.shape, bf),
             pltpu.SMEM(retrieval.shape, jnp.int32),

time: 52 us -> 54.2 us (1.042)
  the two profiles are of different devices: /device:TPU:0 before, /device:TPU:7 now
where the time goes in v4:
time: 54.2 us; the launch traced here: 54.1 us
  Pallas kernels  52.1 us (96%)
  local copies, waits for them, and re-layouts  1.33 us (2%)
  between operations  0.64 us (1%)
    pallas_call x1, Pallas kernels, fused(): pl.pallas_call(kernel, out_shape=(pltpu.VMEM(queries.shape, bf), pltpu.VM...  52.1 us
    unnamed x2, local copies, waits for them, and re-layouts  1.33 us

profile of v4, /device:TPU:7, one launch (start us, length us, event | category | flops | bytes accessed | tf_op | source)
XLA Modules:
  0.0 54.1 jit_solution(8776463527699772230)
XLA Ops:
  0.6 52.1 %blend.1 = (bf16[128,1024]{1,0:T(8,128)(2,1)S(1)}, bf16[128,256]{1,0:T(8,128)(2,1)S(1)}) custom-call(bf16[128,2048]{1,0:T(8,128)(2,1)} %hid.1, bf16[2048,128]{1,0:T(8,128)(2,1)} %wgt.1, bf16[128,1024]{1,0:T(8,128)(2,1)} %q_hbm.1, bf16[8,128,256]{2,1,0:T(8,128)(2,1)} %cache_hbm.1, s32[1,4]{1,0:T(1,128)} %retr_hbm.1, s32[1,2,4]{2,1,0:T(2,128)} %pat_hbm.1), custom_call_target="tpu_custom_call" | custom-call | tf_op jit(solution)/shard_map/blend/pallas_call | solution.py:366
  52.8 0.7 %copy.10 = bf16[128,1024]{1,0:T(8,128)(2,1)} copy(bf16[128,1024]{1,0:T(8,128)(2,1)S(1)} %get-tuple-element.2) | data formatting | bytes 524288
  53.5 0.6 %copy.11 = bf16[128,256]{1,0:T(8,128)(2,1)} copy(bf16[128,256]{1,0:T(8,128)(2,1)S(1)} %get-tuple-element.3) | data formatting | bytes 131072

commit v5 on v4

--- a/solution.py
+++ b/solution.py
@@ -95,7 +95,7 @@
 
 
 def kernel(hid, wgt, q_hbm, cache_hbm, retr_hbm, pat_hbm, att, fresh, hbuf, wbuf, wsrc, pbuf, part,
-           msg_out, msg_in, reply, arrived, top_ref, sum_ref, acc_ref, q_ref, cache, retr, pat,
+           msg_out, msg_in, reply, arrived, top_ref, acc_ref, near_bias, q_ref, cache, retr, pat,
            h_recv, p_send, x_send, f_send, w_recv, w_send, v_send, m_recv, m_send, a_recv, a_send,
            s_recv, s_send, load_sem):
     npool = 8
@@ -237,7 +237,7 @@
         def _():
             w_near[c].wait_send()
 
-        for k in ((6, 7), (2, 3, 1))[c]:
+        for k in ((6, 7), (2, 3, 1, 4, 5))[c]:
             answers[k].start()
 
     for c in halves:
@@ -267,10 +267,8 @@
         h_wait((1 - b) * 2 + 1 - x, c)
     project(1 - b)
 
-    for k, first in ((4, 6), (5, 7)):
-        answers[first].wait_send()
-        answers[k].start()
-
+    token = lax.broadcasted_iota(jnp.int32, (rows, rows), 0)
+    near_bias[...] = jnp.where(token >= lax.broadcasted_iota(jnp.int32, (rows, rows), 1), 0.0, -1e30)
     for kind in range(2):
         total = jnp.zeros((rows, HD), jnp.float32)
         for n in range(4):
@@ -280,58 +278,66 @@
     loads[2].wait()
     loads[3].wait()
 
-    scale = float(HD) ** (-0.5)
-
-    def allowed(k):
+    rate = float(HD) ** (-0.5) * math.log2(math.e)
+    r_blocks = pat.shape[1]
+
+    def bias_of(k, r):
         owner = me if k == 0 else peer(k)
-        token = lax.broadcasted_iota(jnp.int32, (rows, BLK), 0)
-        mask = jnp.zeros((rows, BLK), jnp.int32)
-        for r in range(pat.shape[1]):
-            named = jnp.int32(0)
-            for f in range(fetch):
-                named = named + jnp.where(owners[f] == owner, pat[0, r, f], 0)
-            mask = jnp.where(lax.div(token, RBLK) == r, named, mask)
-        return mask != 0
+        named = jnp.int32(0)
+        for f in range(fetch):
+            named = named + jnp.where(owners[f] == owner, pat[0, r, f], 0)
+        return jnp.where(named != 0, jnp.float32(0.0), jnp.float32(-1e30))
 
     def stage(near, ks, last):
-        @pl.loop(0, q_ref.shape[1] // HD, unroll=2)
-        def _(head):
-            at = pl.ds(pl.multiple_of(head * HD, HD), HD)
-            masks = [allowed(k) for k in ks]
+        biases = [[bias_of(k, r) for r in range(r_blocks)] for k in ks]
+
+        @pl.loop(0, q_ref.shape[1] // (2 * HD), unroll=2)
+        def _(step):
+            ats = [pl.ds(pl.multiple_of(step * 2 * HD + h * HD, HD), HD) for h in range(2)]
             keys = [arrived[k, :, 0:HD] for k in ks]
             vals = [arrived[k, :, HD:2 * HD] for k in ks]
             if near:
-                token = lax.broadcasted_iota(jnp.int32, (rows, rows), 0)
-                masks.append(token >= lax.broadcasted_iota(jnp.int32, (rows, rows), 1))
                 keys.append(fresh[:, 0:HD])
                 vals.append(fresh[:, HD:2 * HD])
-            raw = rows_by_keys(q_ref[:, at], jnp.concatenate(keys, axis=0)) * scale
-            scores = [jnp.where(m, raw[:, n * BLK:(n + 1) * BLK], -1e30) for n, m in enumerate(masks)]
-            top = scores[0]
-            for one in scores[1:]:
-                top = jnp.maximum(top, one)
-            top = jnp.max(top, axis=1, keepdims=True)
-            if not near:
-                before = top_ref[head]
-                top = jnp.maximum(before, top)
-                factor = jnp.exp(before - top)
-            else:
-                top = jnp.broadcast_to(top, (rows, HD))
-            weights = [jnp.exp(one - top) for one in scores]
-            denom = weights[0]
-            for one in weights[1:]:
-                denom = denom + one
-            rounded = jnp.concatenate([w.astype(jnp.bfloat16) for w in weights], axis=1)
-            numer = jnp.dot(rounded, jnp.concatenate(vals, axis=0), preferred_element_type=jnp.float32)
-            if not near:
-                denom = denom + factor * sum_ref[head]
-                numer = numer + factor * acc_ref[head]
-            if last:
-                att[:, at] = (numer / jnp.sum(denom, axis=1, keepdims=True)).astype(jnp.bfloat16)
-            else:
-                top_ref[head] = top
-                sum_ref[head] = denom
-                acc_ref[head] = numer
+            keys = jnp.concatenate(keys, axis=0)
+            vals = jnp.concatenate(vals, axis=0)
+            vals = jnp.concatenate([vals, jnp.ones_like(vals)], axis=1)
+            raw = rows_by_keys(jnp.concatenate([q_ref[:, at] for at in ats], axis=0), keys)
+            rounded, factors = [], []
+            for h in range(2):
+                scores = []
+                for n in range(len(ks)):
+                    scores.append(jnp.concatenate([
+                        raw[h * rows + r * RBLK:h * rows + (r + 1) * RBLK, n * BLK:(n + 1) * BLK] + biases[n][r]
+                        for r in range(r_blocks)
+                    ], axis=0))
+                if near:
+                    scores.append(raw[h * rows:(h + 1) * rows, len(ks) * BLK:] + near_bias[...])
+                top = scores[0]
+                for one in scores[1:]:
+                    top = jnp.maximum(top, one)
+                top = jnp.broadcast_to(jnp.max(top, axis=1, keepdims=True), (rows, HD))
+                if not near:
+                    before = top_ref[2 * step + h]
+                    top = jnp.maximum(before, top)
+                    factors.append(jnp.exp2((before - top) * rate))
+                if not last:
+                    top_ref[2 * step + h] = top
+                rounded.append(jnp.concatenate(
+                    [jnp.exp2((one - top) * rate).astype(jnp.bfloat16) for one in scores], axis=1
+                ))
+            both = jnp.dot(jnp.concatenate(rounded, axis=0), vals, preferred_element_type=jnp.float32)
+            for h in range(2):
+                numer = both[h * rows:(h + 1) * rows, 0:HD]
+                denom = both[h * rows:(h + 1) * rows, HD:2 * HD]
+                if not near:
+                    numer = numer + factors[h] * acc_ref[2 * step + h, :, 0:HD]
+                    denom = denom + factors[h] * acc_ref[2 * step + h, :, HD:2 * HD]
+                if last:
+                    att[:, ats[h]] = (numer / denom).astype(jnp.bfloat16)
+                else:
+                    acc_ref[2 * step + h, :, 0:HD] = numer
+                    acc_ref[2 * step + h, :, HD:2 * HD] = denom
 
     for near, ks, last in ((True, (0, 1, 2, 3), False), (False, (6, 7), False), (False, (4, 5), True)):
         for k in ks:
@@ -344,8 +350,7 @@
         h_fwd[c].wait_send()
     for k in range(1, npool):
         ask[k].wait_send()
-        if k not in (6, 7):
-            answers[k].wait_send()
+        answers[k].wait_send()
     for j in range(4):
         for i in range(2):
             mine = jnp.logical_and(4 * a + j == me, 2 * b + i == t)
@@ -382,8 +387,8 @@
             pltpu.VMEM((8, BLK, width), bf),
             pltpu.VMEM((8, BLK, width), bf),
             pltpu.VMEM((queries.shape[1] // HD, rows, HD), jnp.float32),
-            pltpu.VMEM((queries.shape[1] // HD, rows, HD), jnp.float32),
-            pltpu.VMEM((queries.shape[1] // HD, rows, HD), jnp.float32),
+            pltpu.VMEM((queries.shape[1] // HD, rows, 2 * HD), jnp.float32),
+            pltpu.VMEM((rows, rows), jnp.float32),
             pltpu.VMEM(queries.shape, bf),
             pltpu.VMEM(cache_table.shape, bf),
             pltpu.SMEM(retrieval.shape, jnp.int32),

time: 54.2 us -> 49.9 us (0.921)
  the two profiles are of different devices: /device:TPU:7 before, /device:TPU:0 now
where the time goes in v5:
time: 49.9 us; the launch traced here: 49.7 us
  Pallas kernels  47.7 us (96%)
  local copies, waits for them, and re-layouts  1.33 us (3%)
  between operations  0.64 us (1%)
    pallas_call x1, Pallas kernels, fused(): pl.pallas_call(kernel, out_shape=(pltpu.VMEM(queries.shape, bf), pltpu.VM...  47.7 us
    unnamed x2, local copies, waits for them, and re-layouts  1.33 us

profile of v5, /device:TPU:0, one launch (start us, length us, event | category | flops | bytes accessed | tf_op | source)
XLA Modules:
  0.0 49.7 jit_solution(4548077822717618821)
XLA Ops:
  0.6 47.7 %blend.1 = (bf16[128,1024]{1,0:T(8,128)(2,1)S(1)}, bf16[128,256]{1,0:T(8,128)(2,1)S(1)}) custom-call(bf16[128,2048]{1,0:T(8,128)(2,1)} %hid.1, bf16[2048,128]{1,0:T(8,128)(2,1)} %wgt.1, bf16[128,1024]{1,0:T(8,128)(2,1)} %q_hbm.1, bf16[8,128,256]{2,1,0:T(8,128)(2,1)} %cache_hbm.1, s32[1,4]{1,0:T(1,128)} %retr_hbm.1, s32[1,2,4]{2,1,0:T(2,128)} %pat_hbm.1), custom_call_target="tpu_custom_call" | custom-call | tf_op jit(solution)/shard_map/blend/pallas_call | solution.py:371
  48.4 0.7 %copy.10 = bf16[128,1024]{1,0:T(8,128)(2,1)} copy(bf16[128,1024]{1,0:T(8,128)(2,1)S(1)} %get-tuple-element.2) | data formatting | bytes 524288
  49.1 0.6 %copy.11 = bf16[128,256]{1,0:T(8,128)(2,1)} copy(bf16[128,256]{1,0:T(8,128)(2,1)S(1)} %get-tuple-element.3) | data formatting | bytes 131072

commit v6 on v5

--- a/solution.py
+++ b/solution.py
@@ -167,10 +167,25 @@
                 barrier, inc=1,
                 device_id={"pool": (2 * a + y) * 2 + sx, "tp": lax.rem(t + k, 4)}, device_id_type=MESH,
             )
+    loads[0].wait()
+
+    wanted = [retr[0, f] for f in range(fetch)]
+    owners = [lax.div(v, blocks_dev) for v in wanted]
+    locals_ = [lax.rem(v, blocks_dev) for v in wanted]
+
+    def slot_at(owner):
+        total = jnp.int32(0)
+        for f in range(fetch):
+            total = total + jnp.where(owners[f] == owner, locals_[f], 0)
+        return total
+
+    ask, answers = [None], [None]
+    for k in range(1, npool):
+        msg_out[k] = jnp.full((8, 128), slot_at(peer(k)), jnp.int32)
+        ask.append(remote(msg_out.at[k], msg_in.at[k], m_send.at[k], m_recv.at[k], peer(k)))
     for c in halves:
         own_h[c].wait()
     loads[4].wait()
-    loads[0].wait()
     pl.semaphore_wait(barrier, npool - 1 + jnp.where(y == b, 4, 8))
 
     h_pair = [remote(h_part[c], hbuf.at[half_at(own_slot, c)], p_send.at[c], h_recv.at[own_slot, c], pair) for c in halves]
@@ -182,6 +197,8 @@
     w_far = [remote(w_part[c], w_land[c], w_send.at[c], w_recv.at[b, c], far) for c in halves]
     w_near = [remote(w_part[c], w_land[c], v_send.at[c], w_recv.at[b, c], pair) for c in halves]
 
+    for k in range(1, npool):
+        ask[k].start()
     for c in halves:
         h_pair[c].start()
     for c in halves:
@@ -192,28 +209,6 @@
         for c in halves:
             w_far[c].start()
 
-    wanted = [retr[0, f] for f in range(fetch)]
-    owners = [lax.div(v, blocks_dev) for v in wanted]
-    locals_ = [lax.rem(v, blocks_dev) for v in wanted]
-
-    def slot_at(owner):
-        total = jnp.int32(0)
-        for f in range(fetch):
-            total = total + jnp.where(owners[f] == owner, locals_[f], 0)
-        return total
-
-    ask, answers = [None], [None]
-    for k in range(1, npool):
-        msg_out[k] = jnp.full((8, 128), slot_at(peer(k)), jnp.int32)
-        ask.append(remote(msg_out.at[k], msg_in.at[k], m_send.at[k], m_recv.at[k], peer(k)))
-        ask[k].start()
-    loads[1].wait()
-    arrived[0] = cache[slot_at(me)]
-    for k in range(1, npool):
-        ask[k].wait_recv()
-        reply[k] = cache[jnp.max(msg_in[k])]
-        answers.append(remote(reply.at[k], arrived.at[k], a_send.at[k], a_recv.at[k], peer(k)))
-
     def h_wait(slot, c):
         pltpu.make_async_copy(h_in[c], hbuf.at[half_at(slot, c)], h_recv.at[slot, c]).wait()
 
@@ -230,6 +225,13 @@
 
         h_wait(pair_slot, c)
         h_fwd[c].start()
+        if c == 0:
+            loads[1].wait()
+            arrived[0] = cache[slot_at(me)]
+            for k in range(1, npool):
+                ask[k].wait_recv()
+                reply[k] = cache[jnp.max(msg_in[k])]
+                answers.append(remote(reply.at[k], arrived.at[k], a_send.at[k], a_recv.at[k], peer(k)))
     for c in halves:
         w_far[c].wait_send()
 
@@ -237,16 +239,20 @@
         def _():
             w_near[c].wait_send()
 
-        for k in ((6, 7), (2, 3, 1, 4, 5))[c]:
+        for k in ((6, 7), (2, 3, 1))[c]:
             answers[k].start()
 
-    for c in halves:
-        h_wait(b * 2 + 1 - x, c)
-        for s in range(2):
-            pltpu.make_async_copy(w_part[c], wbuf.at[pl.ds(c * half_depth, half_depth), pl.ds(s * HD, HD)], w_recv.at[s, c]).wait()
-
-    def project(zl):
-        block = jnp.dot(hbuf[rows_at(zl * 2, 2)], wbuf[...], preferred_element_type=jnp.float32)
+    def w_wait(c):
+        for n in range(2):
+            pltpu.make_async_copy(
+                w_in[c], wbuf.at[pl.ds(c * half_depth, half_depth), pl.ds(n * HD, HD)], w_recv.at[n, c]
+            ).wait()
+
+    def product(zl, c):
+        at = pl.ds(c * half_depth, half_depth)
+        return jnp.dot(hbuf[rows_at(zl * 2, 2), at], wbuf[at, :], preferred_element_type=jnp.float32)
+
+    def hand_out(zl, block):
         for sx in range(2):
             for i in range(2):
                 j = zl * 2 + sx
@@ -262,19 +268,20 @@
                 def _():
                     remote(src, part.at[x, t], s_send.at[j, i], s_recv.at[x, t], 4 * a + j, 2 * b + i).start()
 
-    project(b)
+    for c in halves:
+        h_wait(b * 2 + 1 - x, c)
+    w_wait(0)
+    first = product(b, 0)
+    w_wait(1)
+    hand_out(b, first + product(b, 1))
     for c in halves:
         h_wait((1 - b) * 2 + 1 - x, c)
-    project(1 - b)
+    hand_out(1 - b, product(1 - b, 0) + product(1 - b, 1))
+    for k in (4, 5):
+        answers[k].start()
 
     token = lax.broadcasted_iota(jnp.int32, (rows, rows), 0)
     near_bias[...] = jnp.where(token >= lax.broadcasted_iota(jnp.int32, (rows, rows), 1), 0.0, -1e30)
-    for kind in range(2):
-        total = jnp.zeros((rows, HD), jnp.float32)
-        for n in range(4):
-            pltpu.make_async_copy(pbuf.at[0, 0], part.at[kind, n], s_recv.at[kind, n]).wait()
-            total = total + part[kind, n].astype(jnp.float32)
-        fresh[:, kind * HD:(kind + 1) * HD] = total.astype(jnp.bfloat16)
     loads[2].wait()
     loads[3].wait()
 
@@ -288,7 +295,7 @@
             named = named + jnp.where(owners[f] == owner, pat[0, r, f], 0)
         return jnp.where(named != 0, jnp.float32(0.0), jnp.float32(-1e30))
 
-    def stage(near, ks, last):
+    def stage(first, near, ks, last):
         biases = [[bias_of(k, r) for r in range(r_blocks)] for k in ks]
 
         @pl.loop(0, q_ref.shape[1] // (2 * HD), unroll=2)
@@ -317,7 +324,7 @@
                 for one in scores[1:]:
                     top = jnp.maximum(top, one)
                 top = jnp.broadcast_to(jnp.max(top, axis=1, keepdims=True), (rows, HD))
-                if not near:
+                if not first:
                     before = top_ref[2 * step + h]
                     top = jnp.maximum(before, top)
                     factors.append(jnp.exp2((before - top) * rate))
@@ -330,7 +337,7 @@
             for h in range(2):
                 numer = both[h * rows:(h + 1) * rows, 0:HD]
                 denom = both[h * rows:(h + 1) * rows, HD:2 * HD]
-                if not near:
+                if not first:
                     numer = numer + factors[h] * acc_ref[2 * step + h, :, 0:HD]
                     denom = denom + factors[h] * acc_ref[2 * step + h, :, HD:2 * HD]
                 if last:
@@ -339,11 +346,21 @@
                     acc_ref[2 * step + h, :, 0:HD] = numer
                     acc_ref[2 * step + h, :, HD:2 * HD] = denom
 
-    for near, ks, last in ((True, (0, 1, 2, 3), False), (False, (6, 7), False), (False, (4, 5), True)):
-        for k in ks:
-            if k:
-                answers[k].wait_recv()
-        stage(near, ks, last)
+    for k in (1, 2, 3):
+        answers[k].wait_recv()
+    stage(True, False, (0, 1, 2, 3), False)
+    for kind in range(2):
+        total = jnp.zeros((rows, HD), jnp.float32)
+        for n in range(4):
+            pltpu.make_async_copy(pbuf.at[0, 0], part.at[kind, n], s_recv.at[kind, n]).wait()
+            total = total + part[kind, n].astype(jnp.float32)
+        fresh[:, kind * HD:(kind + 1) * HD] = total.astype(jnp.bfloat16)
+    for k in (6, 7):
+        answers[k].wait_recv()
+    stage(False, True, (6, 7), False)
+    for k in (4, 5):
+        answers[k].wait_recv()
+    stage(False, False, (4, 5), True)
 
     for c in halves:
         h_other[c].wait_send()

time: 49.9 us -> 45.4 us (0.910)
  the two profiles are of different devices: /device:TPU:0 before, /device:TPU:8 now
where the time goes in v6:
time: 45.4 us; the launch traced here: 45.2 us
  Pallas kernels  43.3 us (95%)
  local copies, waits for them, and re-layouts  1.33 us (3%)
  between operations  0.64 us (1%)
    pallas_call x1, Pallas kernels, fused(): pl.pallas_call(kernel, out_shape=(pltpu.VMEM(queries.shape, bf), pltpu.VM...  43.3 us
    unnamed x2, local copies, waits for them, and re-layouts  1.33 us

profile of v6, /device:TPU:8, one launch (start us, length us, event | category | flops | bytes accessed | tf_op | source)
XLA Modules:
  0.0 45.2 jit_solution(17942609163754214548)
XLA Ops:
  0.6 43.3 %blend.1 = (bf16[128,1024]{1,0:T(8,128)(2,1)S(1)}, bf16[128,256]{1,0:T(8,128)(2,1)S(1)}) custom-call(bf16[128,2048]{1,0:T(8,128)(2,1)} %hid.1, bf16[2048,128]{1,0:T(8,128)(2,1)} %wgt.1, bf16[128,1024]{1,0:T(8,128)(2,1)} %q_hbm.1, bf16[8,128,256]{2,1,0:T(8,128)(2,1)} %cache_hbm.1, s32[1,4]{1,0:T(1,128)} %retr_hbm.1, s32[1,2,4]{2,1,0:T(2,128)} %pat_hbm.1), custom_call_target="tpu_custom_call" | custom-call | tf_op jit(solution)/shard_map/blend/pallas_call | solution.py:388
  43.9 0.7 %copy.10 = bf16[128,1024]{1,0:T(8,128)(2,1)} copy(bf16[128,1024]{1,0:T(8,128)(2,1)S(1)} %get-tuple-element.2) | data formatting | bytes 524288
  44.6 0.6 %copy.11 = bf16[128,256]{1,0:T(8,128)(2,1)} copy(bf16[128,256]{1,0:T(8,128)(2,1)S(1)} %get-tuple-element.3) | data formatting | bytes 131072

commit v7 on v6

--- a/solution.py
+++ b/solution.py
@@ -239,7 +239,7 @@
         def _():
             w_near[c].wait_send()
 
-        for k in ((6, 7), (2, 3, 1))[c]:
+        for k in ((6,), (4, 2))[c]:
             answers[k].start()
 
     def w_wait(c):
@@ -277,7 +277,7 @@
     for c in halves:
         h_wait((1 - b) * 2 + 1 - x, c)
     hand_out(1 - b, product(1 - b, 0) + product(1 - b, 1))
-    for k in (4, 5):
+    for k in (7, 5, 3, 1):
         answers[k].start()
 
     token = lax.broadcasted_iota(jnp.int32, (rows, rows), 0)
@@ -346,21 +346,21 @@
                     acc_ref[2 * step + h, :, 0:HD] = numer
                     acc_ref[2 * step + h, :, HD:2 * HD] = denom
 
-    for k in (1, 2, 3):
+    for k in (2, 6, 4):
         answers[k].wait_recv()
-    stage(True, False, (0, 1, 2, 3), False)
+    stage(True, False, (0, 2, 6, 4), False)
     for kind in range(2):
         total = jnp.zeros((rows, HD), jnp.float32)
         for n in range(4):
             pltpu.make_async_copy(pbuf.at[0, 0], part.at[kind, n], s_recv.at[kind, n]).wait()
             total = total + part[kind, n].astype(jnp.float32)
         fresh[:, kind * HD:(kind + 1) * HD] = total.astype(jnp.bfloat16)
-    for k in (6, 7):
+    for k in (1, 3):
         answers[k].wait_recv()
-    stage(False, True, (6, 7), False)
-    for k in (4, 5):
+    stage(False, True, (1, 3), False)
+    for k in (7, 5):
         answers[k].wait_recv()
-    stage(False, False, (4, 5), True)
+    stage(False, False, (7, 5), True)
 
     for c in halves:
         h_other[c].wait_send()

time: 45.4 us -> 46.8 us (1.031)
  the two profiles are of different devices: /device:TPU:8 before, /device:TPU:0 now
where the time goes in v7:
time: 46.8 us; the launch traced here: 46.6 us
  Pallas kernels  44.7 us (96%)
  local copies, waits for them, and re-layouts  1.33 us (3%)
  between operations  0.64 us (1%)
    pallas_call x1, Pallas kernels, fused(): pl.pallas_call(kernel, out_shape=(pltpu.VMEM(queries.shape, bf), pltpu.VM...  44.7 us
    unnamed x2, local copies, waits for them, and re-layouts  1.33 us

profile of v7, /device:TPU:0, one launch (start us, length us, event | category | flops | bytes accessed | tf_op | source)
XLA Modules:
  0.0 46.6 jit_solution(14359965844642444818)
XLA Ops:
  0.6 44.7 %blend.1 = (bf16[128,1024]{1,0:T(8,128)(2,1)S(1)}, bf16[128,256]{1,0:T(8,128)(2,1)S(1)}) custom-call(bf16[128,2048]{1,0:T(8,128)(2,1)} %hid.1, bf16[2048,128]{1,0:T(8,128)(2,1)} %wgt.1, bf16[128,1024]{1,0:T(8,128)(2,1)} %q_hbm.1, bf16[8,128,256]{2,1,0:T(8,128)(2,1)} %cache_hbm.1, s32[1,4]{1,0:T(1,128)} %retr_hbm.1, s32[1,2,4]{2,1,0:T(2,128)} %pat_hbm.1), custom_call_target="tpu_custom_call" | custom-call | tf_op jit(solution)/shard_map/blend/pallas_call | solution.py:388
  45.3 0.7 %copy.10 = bf16[128,1024]{1,0:T(8,128)(2,1)} copy(bf16[128,1024]{1,0:T(8,128)(2,1)S(1)} %get-tuple-element.2) | data formatting | bytes 524288
  46.0 0.6 %copy.11 = bf16[128,256]{1,0:T(8,128)(2,1)} copy(bf16[128,256]{1,0:T(8,128)(2,1)S(1)} %get-tuple-element.3) | data formatting | bytes 131072

commit v8 on v6

--- a/solution.py
+++ b/solution.py
@@ -239,7 +239,7 @@
         def _():
             w_near[c].wait_send()
 
-        for k in ((6, 7), (2, 3, 1))[c]:
+        for k in ((6, 7), (2, 3, 1, 4))[c]:
             answers[k].start()
 
     def w_wait(c):
@@ -277,8 +277,7 @@
     for c in halves:
         h_wait((1 - b) * 2 + 1 - x, c)
     hand_out(1 - b, product(1 - b, 0) + product(1 - b, 1))
-    for k in (4, 5):
-        answers[k].start()
+    answers[5].start()
 
     token = lax.broadcasted_iota(jnp.int32, (rows, rows), 0)
     near_bias[...] = jnp.where(token >= lax.broadcasted_iota(jnp.int32, (rows, rows), 1), 0.0, -1e30)
@@ -355,12 +354,11 @@
             pltpu.make_async_copy(pbuf.at[0, 0], part.at[kind, n], s_recv.at[kind, n]).wait()
             total = total + part[kind, n].astype(jnp.float32)
         fresh[:, kind * HD:(kind + 1) * HD] = total.astype(jnp.bfloat16)
-    for k in (6, 7):
+    for k in (6, 7, 4):
         answers[k].wait_recv()
-    stage(False, True, (6, 7), False)
-    for k in (4, 5):
-        answers[k].wait_recv()
-    stage(False, False, (4, 5), True)
+    stage(False, True, (6, 7, 4), False)
+    answers[5].wait_recv()
+    stage(False, False, (5,), True)
 
     for c in halves:
         h_other[c].wait_send()

time: 45.4 us -> 45.7 us (level)
  the two profiles are of different devices: /device:TPU:8 before, /device:TPU:0 now
where the time goes in v8:
time: 45.7 us; the launch traced here: 45.5 us
  Pallas kernels  43.6 us (95%)
  local copies, waits for them, and re-layouts  1.33 us (3%)
  between operations  0.64 us (1%)
    pallas_call x1, Pallas kernels, fused(): pl.pallas_call(kernel, out_shape=(pltpu.VMEM(queries.shape, bf), pltpu.VM...  43.6 us
    unnamed x2, local copies, waits for them, and re-layouts  1.33 us

profile of v8, /device:TPU:0, one launch (start us, length us, event | category | flops | bytes accessed | tf_op | source)
XLA Modules:
  0.0 45.5 jit_solution(13068398314426136039)
XLA Ops:
  0.6 43.6 %blend.1 = (bf16[128,1024]{1,0:T(8,128)(2,1)S(1)}, bf16[128,256]{1,0:T(8,128)(2,1)S(1)}) custom-call(bf16[128,2048]{1,0:T(8,128)(2,1)} %hid.1, bf16[2048,128]{1,0:T(8,128)(2,1)} %wgt.1, bf16[128,1024]{1,0:T(8,128)(2,1)} %q_hbm.1, bf16[8,128,256]{2,1,0:T(8,128)(2,1)} %cache_hbm.1, s32[1,4]{1,0:T(1,128)} %retr_hbm.1, s32[1,2,4]{2,1,0:T(2,128)} %pat_hbm.1), custom_call_target="tpu_custom_call" | custom-call | tf_op jit(solution)/shard_map/blend/pallas_call | solution.py:386
  44.2 0.7 %copy.10 = bf16[128,1024]{1,0:T(8,128)(2,1)} copy(bf16[128,1024]{1,0:T(8,128)(2,1)S(1)} %get-tuple-element.2) | data formatting | bytes 524288
  44.9 0.6 %copy.11 = bf16[128,256]{1,0:T(8,128)(2,1)} copy(bf16[128,256]{1,0:T(8,128)(2,1)S(1)} %get-tuple-element.3) | data formatting | bytes 131072

commit v9 on v6

--- a/solution.py
+++ b/solution.py
@@ -239,7 +239,7 @@
         def _():
             w_near[c].wait_send()
 
-        for k in ((6, 7), (2, 3, 1))[c]:
+        for k in ((), (6, 7, 1))[c]:
             answers[k].start()
 
     def w_wait(c):
@@ -273,11 +273,11 @@
     w_wait(0)
     first = product(b, 0)
     w_wait(1)
-    hand_out(b, first + product(b, 1))
     for c in halves:
         h_wait((1 - b) * 2 + 1 - x, c)
     hand_out(1 - b, product(1 - b, 0) + product(1 - b, 1))
-    for k in (4, 5):
+    hand_out(b, first + product(b, 1))
+    for k in (2, 3, 4, 5):
         answers[k].start()
 
     token = lax.broadcasted_iota(jnp.int32, (rows, rows), 0)
@@ -346,18 +346,18 @@
                     acc_ref[2 * step + h, :, 0:HD] = numer
                     acc_ref[2 * step + h, :, HD:2 * HD] = denom
 
-    for k in (1, 2, 3):
+    for k in (1, 6, 7):
         answers[k].wait_recv()
-    stage(True, False, (0, 1, 2, 3), False)
+    stage(True, False, (0, 1, 6, 7), False)
     for kind in range(2):
         total = jnp.zeros((rows, HD), jnp.float32)
         for n in range(4):
             pltpu.make_async_copy(pbuf.at[0, 0], part.at[kind, n], s_recv.at[kind, n]).wait()
             total = total + part[kind, n].astype(jnp.float32)
         fresh[:, kind * HD:(kind + 1) * HD] = total.astype(jnp.bfloat16)
-    for k in (6, 7):
+    for k in (2, 3):
         answers[k].wait_recv()
-    stage(False, True, (6, 7), False)
+    stage(False, True, (2, 3), False)
     for k in (4, 5):
         answers[k].wait_recv()
     stage(False, False, (4, 5), True)

time: 45.4 us -> 48 us (1.057)
  the two profiles are of different devices: /device:TPU:8 before, /device:TPU:0 now
where the time goes in v9:
time: 48 us; the launch traced here: 47.9 us
  Pallas kernels  45.9 us (96%)
  local copies, waits for them, and re-layouts  1.33 us (3%)
  between operations  0.64 us (1%)
    pallas_call x1, Pallas kernels, fused(): pl.pallas_call(kernel, out_shape=(pltpu.VMEM(queries.shape, bf), pltpu.VM...  45.9 us
    unnamed x2, local copies, waits for them, and re-layouts  1.33 us

profile of v9, /device:TPU:0, one launch (start us, length us, event | category | flops | bytes accessed | tf_op | source)
XLA Modules:
  0.0 47.9 jit_solution(10321116556618321556)
XLA Ops:
  0.6 45.9 %blend.1 = (bf16[128,1024]{1,0:T(8,128)(2,1)S(1)}, bf16[128,256]{1,0:T(8,128)(2,1)S(1)}) custom-call(bf16[128,2048]{1,0:T(8,128)(2,1)} %hid.1, bf16[2048,128]{1,0:T(8,128)(2,1)} %wgt.1, bf16[128,1024]{1,0:T(8,128)(2,1)} %q_hbm.1, bf16[8,128,256]{2,1,0:T(8,128)(2,1)} %cache_hbm.1, s32[1,4]{1,0:T(1,128)} %retr_hbm.1, s32[1,2,4]{2,1,0:T(2,128)} %pat_hbm.1), custom_call_target="tpu_custom_call" | custom-call | tf_op jit(solution)/shard_map/blend/pallas_call | solution.py:388
  46.5 0.7 %copy.10 = bf16[128,1024]{1,0:T(8,128)(2,1)} copy(bf16[128,1024]{1,0:T(8,128)(2,1)S(1)} %get-tuple-element.2) | data formatting | bytes 524288
  47.2 0.6 %copy.11 = bf16[128,256]{1,0:T(8,128)(2,1)} copy(bf16[128,256]{1,0:T(8,128)(2,1)S(1)} %get-tuple-element.3) | data formatting | bytes 131072

commit v10 on v8

--- a/solution.py
+++ b/solution.py
@@ -348,17 +348,17 @@
     for k in (1, 2, 3):
         answers[k].wait_recv()
     stage(True, False, (0, 1, 2, 3), False)
+    for k in (6, 7, 4):
+        answers[k].wait_recv()
+    stage(False, False, (6, 7, 4), False)
     for kind in range(2):
         total = jnp.zeros((rows, HD), jnp.float32)
         for n in range(4):
             pltpu.make_async_copy(pbuf.at[0, 0], part.at[kind, n], s_recv.at[kind, n]).wait()
             total = total + part[kind, n].astype(jnp.float32)
         fresh[:, kind * HD:(kind + 1) * HD] = total.astype(jnp.bfloat16)
-    for k in (6, 7, 4):
-        answers[k].wait_recv()
-    stage(False, True, (6, 7, 4), False)
     answers[5].wait_recv()
-    stage(False, False, (5,), True)
+    stage(False, True, (5,), True)
 
     for c in halves:
         h_other[c].wait_send()

time: 45.7 us -> 45.8 us (level)
  no operation moved by 1% of the time
where the time goes in v10:
time: 45.8 us; the launch traced here: 45.6 us
  Pallas kernels  43.6 us (95%)
  local copies, waits for them, and re-layouts  1.33 us (3%)
  between operations  0.64 us (1%)
    pallas_call x1, Pallas kernels, fused(): pl.pallas_call(kernel, out_shape=(pltpu.VMEM(queries.shape, bf), pltpu.VM...  43.6 us
    unnamed x2, local copies, waits for them, and re-layouts  1.33 us

profile of v10, /device:TPU:0, one launch (start us, length us, event | category | flops | bytes accessed | tf_op | source)
XLA Modules:
  0.0 45.6 jit_solution(8798932180759099274)
XLA Ops:
  0.6 43.6 %blend.1 = (bf16[128,1024]{1,0:T(8,128)(2,1)S(1)}, bf16[128,256]{1,0:T(8,128)(2,1)S(1)}) custom-call(bf16[128,2048]{1,0:T(8,128)(2,1)} %hid.1, bf16[2048,128]{1,0:T(8,128)(2,1)} %wgt.1, bf16[128,1024]{1,0:T(8,128)(2,1)} %q_hbm.1, bf16[8,128,256]{2,1,0:T(8,128)(2,1)} %cache_hbm.1, s32[1,4]{1,0:T(1,128)} %retr_hbm.1, s32[1,2,4]{2,1,0:T(2,128)} %pat_hbm.1), custom_call_target="tpu_custom_call" | custom-call | tf_op jit(solution)/shard_map/blend/pallas_call | solution.py:386
  44.3 0.7 %copy.10 = bf16[128,1024]{1,0:T(8,128)(2,1)} copy(bf16[128,1024]{1,0:T(8,128)(2,1)S(1)} %get-tuple-element.2) | data formatting | bytes 524288
  45.0 0.6 %copy.11 = bf16[128,256]{1,0:T(8,128)(2,1)} copy(bf16[128,256]{1,0:T(8,128)(2,1)S(1)} %get-tuple-element.3) | data formatting | bytes 131072

commit v11 on v10

--- a/solution.py
+++ b/solution.py
@@ -239,7 +239,7 @@
         def _():
             w_near[c].wait_send()
 
-        for k in ((6, 7), (2, 3, 1, 4))[c]:
+        for k in ((6, 7), (2, 3, 1, 4, 5))[c]:
             answers[k].start()
 
     def w_wait(c):
@@ -277,7 +277,6 @@
     for c in halves:
         h_wait((1 - b) * 2 + 1 - x, c)
     hand_out(1 - b, product(1 - b, 0) + product(1 - b, 1))
-    answers[5].start()
 
     token = lax.broadcasted_iota(jnp.int32, (rows, rows), 0)
     near_bias[...] = jnp.where(token >= lax.broadcasted_iota(jnp.int32, (rows, rows), 1), 0.0, -1e30)

time: 45.8 us -> 46.7 us (1.020)
  Pallas kernels: 43.6 us -> 44.6 us
    pallas_call x1, Pallas kernels: 43.6 us -> 44.6 us  [fused(): pl.pallas_call(kernel, out_shape=(pltpu.VMEM(queries.shape, bf), pltpu.VM...]
where the time goes in v11:
time: 46.7 us; the launch traced here: 46.6 us
  Pallas kernels  44.6 us (96%)
  local copies, waits for them, and re-layouts  1.33 us (3%)
  between operations  0.64 us (1%)
    pallas_call x1, Pallas kernels, fused(): pl.pallas_call(kernel, out_shape=(pltpu.VMEM(queries.shape, bf), pltpu.VM...  44.6 us
    unnamed x2, local copies, waits for them, and re-layouts  1.33 us

profile of v11, /device:TPU:0, one launch (start us, length us, event | category | flops | bytes accessed | tf_op | source)
XLA Modules:
  0.0 46.6 jit_solution(3737293210756147761)
XLA Ops:
  0.6 44.6 %blend.1 = (bf16[128,1024]{1,0:T(8,128)(2,1)S(1)}, bf16[128,256]{1,0:T(8,128)(2,1)S(1)}) custom-call(bf16[128,2048]{1,0:T(8,128)(2,1)} %hid.1, bf16[2048,128]{1,0:T(8,128)(2,1)} %wgt.1, bf16[128,1024]{1,0:T(8,128)(2,1)} %q_hbm.1, bf16[8,128,256]{2,1,0:T(8,128)(2,1)} %cache_hbm.1, s32[1,4]{1,0:T(1,128)} %retr_hbm.1, s32[1,2,4]{2,1,0:T(2,128)} %pat_hbm.1), custom_call_target="tpu_custom_call" | custom-call | tf_op jit(solution)/shard_map/blend/pallas_call | solution.py:385
  45.2 0.7 %copy.10 = bf16[128,1024]{1,0:T(8,128)(2,1)} copy(bf16[128,1024]{1,0:T(8,128)(2,1)S(1)} %get-tuple-element.2) | data formatting | bytes 524288
  46.0 0.6 %copy.11 = bf16[128,256]{1,0:T(8,128)(2,1)} copy(bf16[128,256]{1,0:T(8,128)(2,1)S(1)} %get-tuple-element.3) | data formatting | bytes 131072
